TPU v7x, 32 devices: a whole 2x2x4 slice. The times are simulated.
32 devices in a mesh: dp: 4 (over z), expert: 8 (over y, x, core).
Axes of the slice: x: 2, y: 2, z: 4, core: 2. Of those that a mesh axis runs over, the one named last changes fastest.
Arguments:
- tokens: bfloat16 [30976, 768], P(('dp', 'expert')), may hold values from -6 to 6
- first_gain: float32 [768], replicated, may hold values from 0.5 to 1.5
- first_shift: float32 [768], replicated, may hold values from -0.6 to 0.6
- query_weight: bfloat16 [768, 768], replicated, may hold values from -0.21875 to 0.21875
- query_bias: float32 [768], replicated, may hold values from -0.6 to 0.6
- key_weight: bfloat16 [768, 768], replicated, may hold values from -0.21875 to 0.21875
- value_weight: bfloat16 [768, 768], replicated, may hold values from -0.21875 to 0.21875
- value_bias: float32 [768], replicated, may hold values from -0.6 to 0.6
- out_weight: bfloat16 [768, 768], replicated, may hold values from -3.5 to 3.5
- out_bias: float32 [768], replicated, may hold values from -0.6 to 0.6
- second_gain: float32 [768], replicated, may hold values from 0.5 to 1.5
- second_shift: float32 [768], replicated, may hold values from -0.6 to 0.6
- router: bfloat16 [768, 8], replicated, may hold values from -0.15625 to 0.15625
- expert_up: bfloat16 [8, 768, 3072], P('expert'), may hold values from -0.21875 to 0.21875
- expert_up_bias: float32 [8, 3072], P('expert'), may hold values from -0.6 to 0.6
- expert_down: bfloat16 [8, 3072, 768], P('expert'), may hold values from -1.75 to 1.75
- expert_down_bias: float32 [8, 768], P('expert'), may hold values from -6 to 6
- choices: int32 [30976, 2], P(('dp', 'expert')), may hold values from 0 to 7, all different within a row; in each aligned block of 968 rows (0 to 967, 968 to 1935, ...) at most 384 rows name the same one
- priority: int32 [32, 968], P(('dp', 'expert')), may hold values from 0 to 967, each once within a row
- cotangent: bfloat16 [30976, 768], P(('dp', 'expert')), may hold values from -6 to 6
Outputs:
- block_output: bfloat16 [30976, 768], P(('dp', 'expert'))
- input_grad: bfloat16 [30976, 768], P(('dp', 'expert'))
- first_gain_grad: float32 [768], replicated
- first_shift_grad: float32 [768], replicated
- query_weight_grad: float32 [768, 768], replicated
- query_bias_grad: float32 [768], replicated
- key_weight_grad: float32 [768, 768], replicated
- value_weight_grad: float32 [768, 768], replicated
- value_bias_grad: float32 [768], replicated
- out_weight_grad: float32 [768, 768], replicated
- out_bias_grad: float32 [768], replicated
- second_gain_grad: float32 [768], replicated
- second_shift_grad: float32 [768], replicated
- router_grad: float32 [768, 8], replicated
- expert_up_grad: float32 [8, 768, 3072], P('expert', 'dp')
- expert_up_bias_grad: float32 [8, 3072], P('expert', 'dp')
- expert_down_grad: float32 [8, 3072, 768], P('expert', 'dp')
- expert_down_bias_grad: float32 [8, 768], P('expert', 'dp')
Inputs may be any that keep to these rules, and one draw needn't show every extreme that they name: `choices`: the two experts of a patch differ; among the pairs of one device's patches no expert is named more than 384 times. `priority`: each row holds every number from 0 to 967 once.
All inputs are finite; a program needn't handle non-finite values.
Results may differ from a plain program's by a relative error of at most 0.015.
Values may be sent and summed in bfloat16 or wider, within the bound.
No kernel may reach another device: no remote copies, remote signals or barrier semaphores. Data moves between devices by JAX's collectives and lax.ppermute only.
A program may use at most 320 MiB of HBM per device.

v0:
```python
import functools

import jax
import jax.numpy as jnp
from jax import lax
from jax.experimental import pallas as pl
from jax.experimental.pallas import tpu as pltpu
from jax.sharding import PartitionSpec as P

HEADS = 12
BIG = 576
SMALL = 196
LANES = 128
EXTRA = 16
HEAD_GROUPS = 2

half_type = jnp.bfloat16
full_type = jnp.float32
norm_eps = 1e-06
masked_score = -1000000000.0
vmem_bytes = 56 * 2**20


def dot_full(left, right, dims):
    return lax.dot_general(left, right, (dims, ((), ())), preferred_element_type=full_type)


def mul(left, right):
    return dot_full(left, right, ((1,), (0,)))


def mul_t(left, right):
    return dot_full(left, right, ((1,), (1,)))


def t_mul(left, right):
    return dot_full(left, right, ((0,), (0,)))


def row_blocks(rows, step=256):
    return [(start, min(step, rows - start)) for start in range(0, rows, step)]


def iota(shape, dim):
    return lax.broadcasted_iota(jnp.int32, shape, dim)


def ones_where(mask):
    return jnp.where(mask, 1.0, 0.0).astype(half_type)


def normalize(values):
    row_mean = jnp.mean(values, axis=-1, keepdims=True)
    centered = values - row_mean
    inverse = lax.rsqrt(jnp.mean(centered * centered, axis=-1, keepdims=True) + norm_eps)
    return centered * inverse, inverse


def norm_backward(upstream, normed, inverse, norm_gain):
    scaled = upstream * norm_gain
    first_mean = jnp.mean(scaled, axis=-1, keepdims=True)
    second_mean = jnp.mean(scaled * normed, axis=-1, keepdims=True)
    return inverse * (scaled - first_mean - normed * second_mean)


def split_thirds(values, lane, expert_count):
    high = values.astype(half_type).astype(full_type)
    rest = values - high
    middle = rest.astype(half_type).astype(full_type)
    low = rest - middle
    picked = jnp.where(lane < expert_count, high, jnp.where(lane < 2 * expert_count, middle, low))
    return jnp.where(lane < 3 * expert_count, picked, 0.0).astype(half_type)


def call(body, out_shape, name, after=(), grid=(1,), in_specs=None, flops=1024, **kwargs):
    def build(*operands):
        specs = list(in_specs) if in_specs else [whole(a) for a in operands]
        used = len(specs)
        if "out_specs" not in kwargs:
            kwargs["out_specs"] = jax.tree.map(whole, out_shape)

        def inner(*refs):
            body(*refs[:used], *refs[used + len(after) :])

        return pl.pallas_call(
            inner,
            out_shape=out_shape,
            name=name,
            grid=grid,
            in_specs=specs + [pl.BlockSpec(memory_space=pl.ANY)] * len(after),
            compiler_params=pltpu.CompilerParams(vmem_limit_bytes=vmem_bytes),
            cost_estimate=pl.CostEstimate(flops=flops, bytes_accessed=1024, transcendentals=0),
            **kwargs,
        )(*operands, *after)

    return build


def whole(array):
    zeros = (0,) * len(array.shape)
    return pl.BlockSpec(array.shape, lambda *_: zeros)


def out(shape, dtype):
    return jax.ShapeDtypeStruct(shape, dtype)


def vec(ref):
    return ref[...].reshape(1, -1)


def for_experts(expert_count, step):
    if expert_count <= 8:
        for e in range(expert_count):
            step(e)
    else:
        lax.fori_loop(0, expert_count, lambda e, c: (step(e), c)[1], 0)


def expert_rows(e, capacity):
    if isinstance(e, int):
        return pl.ds(e * capacity, capacity)
    return pl.ds(pl.multiple_of(e * capacity, capacity), capacity)


def row_thirds(row):
    high = row.astype(half_type).astype(full_type)
    rest = row - high
    middle = rest.astype(half_type).astype(full_type)
    sub = iota((8, row.shape[1]), 0)
    picked = jnp.where(sub == 0, high, jnp.where(sub == 1, middle, jnp.where(sub == 2, rest - middle, 0.0)))
    return picked.astype(half_type)


def thirds_to_lanes(thirds):
    return t_mul(thirds, jnp.ones((thirds.shape[0], LANES), half_type))


def store_thirds(ref, start, row):
    ref[pl.ds(start, EXTRA), :] = jnp.zeros((EXTRA, ref.shape[1]), ref.dtype)
    thirds = jnp.concatenate([row_thirds(row), jnp.zeros((EXTRA - 8, row.shape[1]), half_type)], axis=0)
    ref[pl.ds(start, EXTRA), 0 : row.shape[1]] = thirds


def part_start(e, size, offset=0):
    if isinstance(e, int):
        return e * size + offset
    return pl.multiple_of(e * size + offset, 16)


def lanes_to_row(values):
    ones = jnp.ones((8, LANES), half_type)
    high = values.astype(half_type)
    rest = values - high.astype(full_type)
    middle = rest.astype(half_type)
    low = (rest - middle.astype(full_type)).astype(half_type)
    return (mul_t(ones, high) + mul_t(ones, middle) + mul_t(ones, low))[0:1]


def rank_column(rows):
    tok_count = rows.shape[1]
    rows = jnp.concatenate([rows, jnp.zeros((8 - rows.shape[0], tok_count), jnp.int32)], axis=0)
    return rows.astype(full_type).T.astype(jnp.int32)


def route_body(expert_count, capacity, rows_ref, rank_ref, cot_ref, place_ref, sent_ref):
    tok_count = cot_ref.shape[0]
    padded = place_ref.shape[0]
    sub = iota((padded, tok_count), 0)
    first, second = rows_ref[0:1, :], rows_ref[1:2, :]
    first_hot, second_hot = ones_where(first == sub), ones_where(second == sub)
    earlier = ones_where(rank_column(rank_ref[...])[:, 0:1] < rank_ref[...])
    first_total = jnp.sum(first_hot.astype(full_type), axis=1, keepdims=True)
    counts = mul(jnp.concatenate([first_hot, second_hot], axis=0), earlier)
    first_count, second_count = counts[:padded], counts[padded:] + first_total
    place = jnp.where(
        (first == sub) & (first_count < capacity),
        first_count,
        jnp.where((second == sub) & (second_count < capacity), second_count, -1.0),
    )
    place_ref[...] = place.astype(jnp.int32)
    cot = cot_ref[...]
    within = iota((capacity, tok_count), 0)

    def send(e):
        hot = ones_where(place_ref[pl.ds(e, 1), :] == within)
        sent_ref[pl.ds(part_start(e, capacity), capacity), :] = mul(hot, cot).astype(half_type)

    for_experts(expert_count, send)


def route(choice_rows, priority, cotangent, expert_count, capacity):
    tok_count, feat = cotangent.shape
    padded = -(-expert_count // 32) * 32
    return call(
        functools.partial(route_body, expert_count, capacity),
        (out((padded, tok_count), jnp.int32), out((expert_count * capacity, feat), half_type)),
        "route",
    )(choice_rows, priority, cotangent)


def slots_body(capacity, rows_ref, place_ref, slot_ref):
    part = capacity + EXTRA
    padded, tok_count = place_ref.shape
    sub = iota((padded, tok_count), 0)
    slots = []
    for k in range(2):
        place = jnp.sum(jnp.where(rows_ref[k : k + 1, :] == sub, place_ref[...], 0), axis=0, keepdims=True)
        slots.append(jnp.where(place < 0, -1, rows_ref[k : k + 1, :] * part + place))
    slot_ref[...] = rank_column(jnp.concatenate(slots, axis=0))[:, 0:2]


def slot_columns(choice_rows, place, capacity, after):
    return call(
        functools.partial(slots_body, capacity), out((choice_rows.shape[1], 2), jnp.int32), "slot_columns", after
    )(choice_rows, place)


def image_mask(size):
    key_image = iota((size, 1), 0) // SMALL
    query_image = iota((1, size), 1) // SMALL
    return key_image == query_image


def images(tok_count):
    return ((0, BIG), (BIG, tok_count - BIG))


def head_lanes(value, head):
    lane = iota((1, LANES), 1)
    return jnp.where((lane < LANES // 2) == (head == 0), value, jnp.zeros((), value.dtype))


def front_body(
    expert_count,
    capacity,
    tokens_ref,
    gain_ref,
    shift_ref,
    wq_ref,
    bq_ref,
    wk_ref,
    wv_ref,
    bv_ref,
    wo_ref,
    bo_ref,
    gain2_ref,
    shift2_ref,
    router_ref,
    place_ref,
    first_ref,
    q_ref,
    k_ref,
    v_ref,
    log_big_ref,
    log_small_ref,
    attended_ref,
    middle_ref,
    second_ref,
    probs_ref,
    sent_ref,
):
    tok_count, feat = tokens_ref.shape
    scale = (feat // HEADS) ** (-0.5)
    for start, size in row_blocks(tok_count):
        rows = pl.ds(start, size)
        normed, _ = normalize(tokens_ref[rows, :].astype(full_type))
        low = (normed * vec(gain_ref) + vec(shift_ref)).astype(half_type)
        first_ref[rows, :] = low
        q_ref[rows, :] = (mul(low, wq_ref[...]) + vec(bq_ref)).astype(half_type)
        k_ref[rows, :] = mul(low, wk_ref[...]).astype(half_type)
        v_ref[rows, :] = (mul(low, wv_ref[...]) + vec(bv_ref)).astype(half_type)

    def pair(number, carry):
        lanes = pl.ds(pl.multiple_of(number * LANES, LANES), LANES)
        for place, (start, size) in enumerate(images(tok_count)):
            rows = pl.ds(start, size)
            query, key, value = q_ref[rows, lanes], k_ref[rows, lanes], v_ref[rows, lanes]
            key = key * jnp.asarray(scale, half_type)
            log_ref = (log_big_ref, log_small_ref)[place]
            value_t = value.T
            halves = []
            for head in range(2):
                scores = mul_t(head_lanes(key, head), query)
                if place:
                    scores = jnp.where(image_mask(size), scores, masked_score)
                top = jnp.max(scores, axis=0, keepdims=True)
                weights = jnp.exp(scores - top)
                total = jnp.sum(weights, axis=0, keepdims=True)
                log_ref[pl.ds(2 * number + head, 1), :] = top + jnp.log(total)
                mixed = mul(value_t[head * 64 : head * 64 + 64], weights.astype(half_type))
                halves.append(mixed * (1.0 / total))
            attended_ref[rows, lanes] = jnp.concatenate(halves, axis=0).T.astype(half_type)
        return carry

    lax.fori_loop(0, HEADS // 2, pair, 0)

    for start, size in row_blocks(tok_count):
        rows = pl.ds(start, size)
        lane = iota((size, LANES), 1)
        middle = tokens_ref[rows, :].astype(full_type) + mul(attended_ref[rows, :], wo_ref[...]) + vec(bo_ref)
        middle_ref[rows, :] = middle
        normed, _ = normalize(middle)
        low = (normed * vec(gain2_ref) + vec(shift2_ref)).astype(half_type)
        second_ref[rows, :] = low
        logits = jnp.where(lane < 3 * expert_count, mul(low, router_ref[...]), masked_score)
        top = jnp.max(logits, axis=1, keepdims=True)
        raised = jnp.exp(logits - top)
        total = jnp.sum(jnp.where(lane < expert_count, raised, 0.0), axis=1, keepdims=True)
        probs_ref[rows, :] = raised / total

    low = second_ref[...]
    lane = iota((tok_count, LANES), 1)
    thirds = split_thirds(probs_ref[...], lane, expert_count)
    within = iota((capacity, tok_count), 0)
    slot_lane = iota((capacity, LANES), 1)

    def send(e):
        hot = ones_where(place_ref[pl.ds(e, 1), :] == within)
        rows = mul(hot, low).astype(half_type)
        part = capacity + EXTRA
        sent_ref[pl.ds(part_start(e, part), capacity), :] = rows
        gates = mul(hot, thirds)
        own = (slot_lane == e) | (slot_lane == e + expert_count) | (slot_lane == e + 2 * expert_count)
        picked = jnp.where(own, gates, 0.0).astype(half_type)
        store_thirds(sent_ref, part_start(e, part, capacity), mul_t(jnp.ones((8, LANES), half_type), picked)[0:1])

    for_experts(expert_count, send)


def front(tokens, vectors, weights, router3, place, expert_count, capacity):
    tok_count, feat = tokens.shape
    gain, shift, bq, bv, bo, gain2, shift2 = vectors
    wq, wk, wv, wo = weights
    low = out((tok_count, feat), half_type)
    return call(
        functools.partial(front_body, expert_count, capacity),
        (
            low,
            low,
            low,
            low,
            out((HEADS, BIG), full_type),
            out((HEADS, tok_count - BIG), full_type),
            low,
            out((tok_count, feat), full_type),
            low,
            out((tok_count, LANES), full_type),
            out((expert_count * (capacity + EXTRA), feat), half_type),
        ),
        "front",
    )(tokens, gain, shift, wq, bq, wk, wv, bv, wo, bo, gain2, shift2, router3, place)


def fold_lanes(values):
    folded = values[:, :LANES]
    for start in range(LANES, values.shape[1], LANES):
        folded = folded + values[:, start : start + LANES]
    return folded


def act_grad_body(cot_ref, down_ref, down_bias_ref, grad_act_ref, score_ref):
    for start, size in row_blocks(cot_ref.shape[0], 512):
        rows = pl.ds(start, size)
        grad_act_ref[rows, :] = mul_t(cot_ref[rows, :], down_ref[...]).astype(half_type)

        @pl.when(pl.program_id(0) == 0)
        def _():
            score_ref[rows, :] = fold_lanes(cot_ref[rows, :].astype(full_type) * down_bias_ref[...])


def act_grad(cot, down, down_bias, step=512):
    slots, feat = cot.shape
    hidden = down.shape[0]
    return call(
        act_grad_body,
        (out((slots, hidden), half_type), out((slots, LANES), full_type)),
        "act_grad",
        grid=(hidden // step,),
        in_specs=[whole(cot), pl.BlockSpec((step, feat), lambda f: (f, 0)), whole(down_bias)],
        out_specs=[pl.BlockSpec((slots, step), lambda f: (0, f)), pl.BlockSpec((slots, LANES), lambda f: (0, 0))],
    )(cot, down, down_bias)


def gelu_parts(values):
    area = 0.5 + 0.5 * lax.erf(values * 0.7071067811865476)
    bell = jnp.exp(values * values * -0.5) * 0.3989422804014327
    return values * area, area + values * bell


def expert_body(rows_ref, up_ref, up_bias_ref, grad_act_ref, start_ref, cot_ref, act_ref, grad_pre_ref, gate_ref, score_ref, sum_ref, x_ref, gated_ref, grad_ref, bias_ref, up_out_ref, down_out_ref, sems):
    slots, feat = cot_ref.shape
    replicas, share = up_out_ref.shape[1:3]
    steps = (sum_ref.shape[1] - EXTRA) // share // 2
    part = rows_ref.shape[0] // (rows_ref.shape[0] - slots) * EXTRA
    capacity = part - EXTRA
    number = pl.program_id(0)
    down_rows = steps * share
    size = min(down_rows, feat)

    def copies(step):
        pairs = [(up_out_ref.at[step % 2], sum_ref.at[:, pl.ds(step * share, share), :])]
        for piece in range(feat // size):
            row = step * feat + piece * size
            target = sum_ref.at[row // down_rows, pl.ds(down_rows + row % down_rows, size), :]
            pairs.append((down_out_ref.at[step % 2, pl.ds(piece * size, size)], target))
        return [pltpu.make_async_copy(a, b, sems.at[step, i]) for i, (a, b) in enumerate(pairs)]

    @pl.when(number == 0)
    def _():
        total = jnp.zeros((1, feat), full_type)
        for e in range(slots // capacity):
            rows = pl.ds(e * capacity, capacity)
            gate = thirds_to_lanes(rows_ref[pl.ds(e * part + capacity, EXTRA), 0:capacity])
            gate_ref[rows, :] = gate
            wide = jnp.concatenate([gate] * (feat // LANES), axis=1)
            x = rows_ref[pl.ds(e * part, capacity), :]
            x_ref[rows, :] = x
            gated_ref[rows, :] = (x.astype(full_type) * wide).astype(half_type)
            grad = (cot_ref[rows, :].astype(full_type) * wide).astype(half_type)
            grad_ref[rows, :] = grad
            total = total + jnp.sum(grad.astype(full_type), axis=0, keepdims=True)
        bias_ref[...] = jnp.zeros(bias_ref.shape, half_type)
        for z in range(replicas):
            bias_ref[z, 8:9, 0:share] = total[:, z * share : z * share + share].astype(half_type)
        score_ref[...] = start_ref[...]

    blocks = row_blocks(slots, 512)
    pre = mul(x_ref[pl.ds(*blocks[0]), :], up_ref[...])
    bias_grad = jnp.zeros((1, feat), full_type)
    for b, block in enumerate(blocks):
        rows = pl.ds(*block)
        if b + 1 < len(blocks):
            later = mul(x_ref[pl.ds(*blocks[b + 1]), :], up_ref[...])
        act, slope = gelu_parts(pre + up_bias_ref[...])
        act_ref[rows, :] = act.astype(half_type)
        grad_act = grad_act_ref[rows, :].astype(full_type)
        score_ref[rows, :] += fold_lanes(act * grad_act)
        grad_pre_ref[rows, :] = (grad_act * slope).astype(half_type)
        pre = later
    for step in range(2, steps):

        @pl.when(number == step)
        def _():
            for copy in copies(step - 2):
                copy.wait()

    up_out_ref[number % 2] = t_mul(gated_ref[...], grad_pre_ref[...]).astype(half_type).reshape(replicas, share, feat)
    down_out_ref[number % 2] = t_mul(act_ref[...], grad_ref[...]).astype(half_type)
    for start, size_b in blocks:
        rows = pl.ds(start, size_b)
        wide = jnp.concatenate([gate_ref[rows, :]] * (feat // LANES), axis=1)
        bias_grad = bias_grad + jnp.sum(grad_pre_ref[rows, :].astype(full_type) * wide, axis=0, keepdims=True)
    for step in range(steps):

        @pl.when(number == step)
        def _():
            for piece in range(feat // size):
                z = (step * feat + piece * size) // down_rows
                bias_ref[z, 0:1, 0:size] = bias_grad[:, piece * size : piece * size + size].astype(half_type)
            for copy in copies(step):
                copy.start()

    @pl.when(number == steps - 1)
    def _():
        last = pltpu.make_async_copy(bias_ref, sum_ref.at[:, pl.ds(2 * down_rows, EXTRA), :], sems.at[0, 0])
        last.start()
        score_ref[...] = score_ref[...] * gate_ref[...]
        for step in range(steps - 2, steps):
            for copy in copies(step):
                copy.wait()
        last.wait()


def expert(rows, up, up_bias, grad_act, start, cot, replicas):
    slots, feat = cot.shape
    hidden = up.shape[1]
    steps, share = hidden // feat, feat // replicas
    wide = pl.BlockSpec((slots, feat), lambda f: (0, f))
    once = lambda a: pl.BlockSpec(a.shape, lambda f: (0, 0), pipeline_mode=pl.Buffered(1))
    lanes = out((slots, LANES), full_type)
    return call(
        expert_body,
        (
            out((slots, hidden), half_type),
            out((slots, hidden), half_type),
            lanes,
            lanes,
            out((replicas, 2 * steps * share + EXTRA, feat), half_type),
        ),
        "expert",
        grid=(steps,),
        in_specs=[
            once(rows),
            pl.BlockSpec((feat, feat), lambda f: (0, f)),
            pl.BlockSpec((1, feat), lambda f: (0, f)),
            wide,
            once(start),
            once(cot),
        ],
        out_specs=[
            wide,
            wide,
            whole(lanes),
            whole(lanes),
            pl.BlockSpec(memory_space=pl.ANY),
        ],
        scratch_shapes=[
            pltpu.VMEM((slots, feat), half_type),
            pltpu.VMEM((slots, feat), half_type),
            pltpu.VMEM((slots, feat), half_type),
            pltpu.VMEM((replicas, EXTRA, feat), half_type),
            pltpu.VMEM((2, replicas, share, feat), half_type),
            pltpu.VMEM((2, feat, feat), half_type),
            pltpu.SemaphoreType.DMA((steps, 1 + max(1, feat // (steps * share)))),
        ],
    )(rows, up, up_bias, grad_act, start, cot)


def grad_in_body(capacity, grad_pre_ref, up_ref, gate_ref, score_ref, grad_in_ref):
    part = capacity + EXTRA
    size, feat = grad_pre_ref.shape[0], up_ref.shape[0]
    grad = mul_t(grad_pre_ref[...], up_ref[...])
    grad = grad * jnp.concatenate([gate_ref[...]] * (feat // LANES), axis=1)
    for e in range(size // capacity):
        grad_in_ref[pl.ds(e * part, capacity), :] = grad[e * capacity : e * capacity + capacity].astype(half_type)
        store_thirds(grad_in_ref, e * part + capacity, lanes_to_row(score_ref[e * capacity : e * capacity + capacity, :]))


def expert_grad_in(grad_pre, up, gate, score, capacity, after, step=512):
    slots, hidden = grad_pre.shape
    feat = up.shape[0]
    part = capacity + EXTRA
    lanes = pl.BlockSpec((step, LANES), lambda r: (r, 0))
    return call(
        functools.partial(grad_in_body, capacity),
        out((slots // capacity * part, feat), half_type),
        "grad_in",
        after,
        flops=4 * 10**11,
        grid=(slots // step,),
        in_specs=[pl.BlockSpec((step, hidden), lambda r: (r, 0)), whole(up), lanes, lanes],
        out_specs=pl.BlockSpec((step // capacity * part, feat), lambda r: (r, 0)),
    )(grad_pre, up, gate, score)


def result_body(act_ref, down_ref, down_bias_ref, result_ref):
    result_ref[...] = (mul(act_ref[...], down_ref[...]) + down_bias_ref[...]).astype(half_type)


def expert_result(act, down, down_bias, after=(), step=512):
    slots, hidden = act.shape
    feat = down.shape[1]
    return call(
        result_body,
        out((slots, feat), half_type),
        "result",
        after,
        grid=(slots // step,),
        in_specs=[pl.BlockSpec((step, hidden), lambda r: (r, 0)), whole(down), whole(down_bias)],
        out_specs=pl.BlockSpec((step, feat), lambda r: (r, 0)),
    )(act, down, down_bias)


def combine_body(
    expert_count,
    capacity,
    back_ref,
    slot_ref,
    probs_ref,
    middle_ref,
    cot_ref,
    attended_ref,
    wo_ref,
    router_ref,
    gain_ref,
    shift_ref,
    grad_middle_ref,
    grad_attended_ref,
    wo_grad_ref,
    router_grad_ref,
    vector_ref,
):
    tok_count, feat = cot_ref.shape
    slots = back_ref.shape[0]
    part = capacity + EXTRA
    lane = iota((capacity, LANES), 1)
    tables = []
    for e in range(expert_count):
        same = (lane == e) | (lane == e + expert_count) | (lane == e + 2 * expert_count)
        score = thirds_to_lanes(back_ref[pl.ds(e * part + capacity, EXTRA), 0:capacity])
        tables.append(split_thirds(jnp.where(same, score, 0.0), lane, expert_count))
        tables.append(jnp.zeros((EXTRA, LANES), half_type))
    table = jnp.concatenate(tables, axis=0)
    wo_grad = jnp.zeros(wo_grad_ref.shape, full_type)
    router_grad = jnp.zeros(router_grad_ref.shape, full_type)
    gain_grad = jnp.zeros((1, feat), full_type)
    shift_grad = jnp.zeros((1, feat), full_type)
    bias_grad = jnp.zeros((1, feat), full_type)
    for start, size in row_blocks(tok_count):
        rows = pl.ds(start, size)
        number = iota((size, slots), 1)
        hot = ones_where((number == slot_ref[rows, 0:1]) | (number == slot_ref[rows, 1:2]))
        lane = iota((size, LANES), 1)
        folded = mul(hot, table)
        folded = folded + pltpu.roll(folded, LANES - expert_count, 1) + pltpu.roll(folded, LANES - 2 * expert_count, 1)
        probs = jnp.where(lane < expert_count, probs_ref[rows, :], 0.0)
        scores = jnp.where(lane < expert_count, folded, 0.0)
        grad_logits = scores - probs * jnp.sum(scores, axis=1, keepdims=True)
        grad_logits = grad_logits + pltpu.roll(grad_logits, expert_count, 1) + pltpu.roll(grad_logits, 2 * expert_count, 1)
        thirds = split_thirds(grad_logits, lane, expert_count)
        upstream = mul_t(thirds, router_ref[...]) + mul(hot, back_ref[...])
        normed, inverse = normalize(middle_ref[rows, :])
        low = (normed * vec(gain_ref) + vec(shift_ref)).astype(half_type)
        router_grad = router_grad + t_mul(low, thirds)
        gain_grad = gain_grad + jnp.sum(upstream * normed, axis=0, keepdims=True)
        shift_grad = shift_grad + jnp.sum(upstream, axis=0, keepdims=True)
        grad_middle = cot_ref[rows, :].astype(full_type) + norm_backward(upstream, normed, inverse, vec(gain_ref))
        grad_middle_ref[rows, :] = grad_middle
        branch = grad_middle.astype(half_type)
        bias_grad = bias_grad + jnp.sum(branch.astype(full_type), axis=0, keepdims=True)
        grad_attended_ref[rows, :] = mul_t(branch, wo_ref[...]).astype(half_type)
        wo_grad = wo_grad + t_mul(attended_ref[rows, :], branch)
    wo_grad_ref[...] = wo_grad.astype(half_type)
    router_grad = router_grad + pltpu.roll(router_grad, LANES - expert_count, 1) + pltpu.roll(router_grad, LANES - 2 * expert_count, 1)
    router_grad_ref[...] = router_grad
    vector_ref[0:1, :] = gain_grad
    vector_ref[1:2, :] = shift_grad
    vector_ref[2:3, :] = bias_grad


def combine(back, slot, probs, middle, cot, attended, wo, router3, gain, shift, expert_count, capacity, after=()):
    tok_count, feat = cot.shape
    return call(
        functools.partial(combine_body, expert_count, capacity),
        (
            out((tok_count, feat), full_type),
            out((tok_count, feat), half_type),
            out((feat, feat), half_type),
            out((feat, LANES), full_type),
            out((3, feat), full_type),
        ),
        "combine",
        after,
    )(back, slot, probs, middle, cot, attended, wo, router3, gain, shift)


def attention_grad_body(first_head, q_ref, k_ref, v_ref, grad_ref, log_big_ref, log_small_ref, first_ref, dq_ref, dk_ref, dv_ref, weight_ref, bias_ref):
    tok_count, width = q_ref.shape
    scale = 64 ** (-0.5)

    def pair(number, carry):
        lanes = pl.ds(pl.multiple_of(number * LANES, LANES), LANES)
        for place, (start, size) in enumerate(images(tok_count)):
            rows = pl.ds(start, size)
            query, key, value, grad = q_ref[rows, lanes], k_ref[rows, lanes], v_ref[rows, lanes], grad_ref[rows, lanes]
            key = key * jnp.asarray(scale, half_type)
            log_ref = (log_big_ref, log_small_ref)[place]
            key_t = key.T
            halves = []
            grad_value = jnp.zeros((size, LANES), full_type)
            grad_key = jnp.zeros((size, LANES), full_type)
            for head in range(2):
                scores = mul_t(head_lanes(key, head), query)
                if place:
                    scores = jnp.where(image_mask(size), scores, masked_score)
                probs = jnp.exp(scores - log_ref[pl.ds(first_head + 2 * number + head, 1), :])
                grad_probs = mul_t(head_lanes(value, head), grad)
                inner = jnp.sum(grad_probs * probs, axis=0, keepdims=True)
                grad_scores = (probs * (grad_probs - inner)).astype(half_type)
                grad_value = grad_value + mul(probs.astype(half_type), head_lanes(grad, head))
                grad_key = grad_key + mul(grad_scores, head_lanes(query, head))
                halves.append(mul(key_t[head * 64 : head * 64 + 64], grad_scores))
            dv_ref[rows, lanes] = grad_value.astype(half_type)
            dk_ref[rows, lanes] = (grad_key * scale).astype(half_type)
            dq_ref[rows, lanes] = jnp.concatenate(halves, axis=0).T.astype(half_type)
        return carry

    lax.fori_loop(0, width // LANES, pair, 0)
    first = first_ref[...]
    for kind, grad_ref in enumerate((dq_ref, dk_ref, dv_ref)):
        weight_ref[:, kind * width : kind * width + width] = t_mul(first, grad_ref[...]).astype(half_type)
    bias_ref[0:1, :] = jnp.sum(dq_ref[...].astype(full_type), axis=0, keepdims=True)
    bias_ref[1:2, :] = jnp.sum(dv_ref[...].astype(full_type), axis=0, keepdims=True)


def attention_grad(group, q, k, v, grad, log_big, log_small, first, after=()):
    tok_count, feat = q.shape
    width = feat // HEAD_GROUPS
    columns = pl.BlockSpec((tok_count, width), lambda i: (0, group))
    low = out((tok_count, width), half_type)
    grads = out((feat, 3 * width + (LANES if group == HEAD_GROUPS - 1 else 0)), half_type)
    return call(
        functools.partial(attention_grad_body, group * HEADS // HEAD_GROUPS),
        (low, low, low, grads, out((2, width), full_type)),
        f"attention_grad_{group}",
        after,
        in_specs=[columns, columns, columns, columns, whole(log_big), whole(log_small), whole(first)],
    )(q, k, v, grad, log_big, log_small, first)


def input_grad_body(*refs):
    grads = refs[: 3 * HEAD_GROUPS]
    refs = refs[3 * HEAD_GROUPS :]
    wq_ref, wk_ref, wv_ref, tokens_ref, gain_ref, middle_ref, bias_a_ref, bias_b_ref, second_ref, router_ref = refs[:10]
    result_ref, sums_ref = refs[11:]
    tok_count, feat = tokens_ref.shape
    width = feat // HEAD_GROUPS
    gain_grad = jnp.zeros((1, feat), full_type)
    shift_grad = jnp.zeros((1, feat), full_type)
    for start, size in row_blocks(tok_count):
        rows = pl.ds(start, size)
        upstream = jnp.zeros((size, feat), full_type)
        for group in range(HEAD_GROUPS):
            lanes = pl.ds(group * width, width)
            for grad_ref, weight_ref in zip(grads[3 * group : 3 * group + 3], (wq_ref, wk_ref, wv_ref)):
                upstream = upstream + mul_t(grad_ref[rows, :], weight_ref[:, lanes])
        normed, inverse = normalize(tokens_ref[rows, :].astype(full_type))
        gain_grad = gain_grad + jnp.sum(upstream * normed, axis=0, keepdims=True)
        shift_grad = shift_grad + jnp.sum(upstream, axis=0, keepdims=True)
        grad = middle_ref[rows, :] + norm_backward(upstream, normed, inverse, vec(gain_ref))
        result_ref[rows, :] = grad.astype(half_type)
    biases = jnp.concatenate([bias_a_ref[...], bias_b_ref[...]], axis=1)
    vectors = [jnp.zeros((32, feat), full_type), gain_grad, shift_grad, biases, second_ref[...]]
    vectors.append(jnp.zeros((LANES - 39, feat), full_type))
    columns = jnp.concatenate(vectors, axis=0).T
    lane = iota(columns.shape, 1)
    sums_ref[...] = jnp.where(lane < 32, router_ref[...], columns).astype(half_type)


def input_grad(grads, wq, wk, wv, tokens, gain, grad_middle, bias_parts, second_parts, router_part, sums, after):
    tok_count, feat = tokens.shape
    operands = (*grads, wq, wk, wv, tokens, gain, grad_middle, *bias_parts, second_parts, router_part)
    block = sums.shape[1] // LANES - 1
    return call(
        input_grad_body,
        (out((tok_count, feat), half_type), out(sums.shape, half_type)),
        "input_grad",
        after,
        in_specs=[whole(a) for a in operands] + [pl.BlockSpec(memory_space=pl.ANY)],
        out_specs=[pl.BlockSpec((tok_count, feat), lambda i: (0, 0)), pl.BlockSpec((feat, LANES), lambda i: (0, block))],
        input_output_aliases={len(operands): 1},
    )(*operands, sums)


def output_body(expert_count, returned_ref, slot_ref, probs_ref, middle_ref, result_ref):
    tok_count, feat = middle_ref.shape
    slots = returned_ref.shape[0]
    capacity = slots // expert_count
    part = capacity + EXTRA
    place = iota((1, slots), 1)
    number = place // capacity * part + place % capacity
    for start, size in row_blocks(tok_count):
        rows = pl.ds(start, size)
        lane = iota((size, LANES), 1)
        probs = probs_ref[rows, :]
        table = jnp.zeros((size, slots), full_type)
        for k in range(2):
            slot = slot_ref[rows, k : k + 1]
            gate = jnp.sum(jnp.where(lane == slot // part, probs, 0.0), axis=1, keepdims=True)
            table = jnp.where(number == slot, gate, table)
        high = table.astype(half_type)
        low = (table - high.astype(full_type)).astype(half_type)
        mixed = mul(high, returned_ref[...]) + mul(low, returned_ref[...])
        result_ref[rows, :] = (middle_ref[rows, :] + mixed).astype(half_type)


def block_result(returned, slot, probs, middle, expert_count, after=()):
    return call(
        functools.partial(output_body, expert_count), out(middle.shape, half_type), "block_result", after
    )(returned, slot, probs, middle)


def together(values, before=()):
    anywhere = pl.BlockSpec(memory_space=pl.ANY)
    count = len(values)
    call_all = pl.pallas_call(
        lambda *refs: None,
        out_shape=[out(v.shape, v.dtype) for v in values],
        name="together",
        in_specs=[anywhere] * (count + len(before)),
        out_specs=[anywhere] * count,
        input_output_aliases={i: i for i in range(count)},
        cost_estimate=pl.CostEstimate(flops=1024, bytes_accessed=1024, transcendentals=0),
    )
    return list(call_all(*values, *before))


def behind(values, *before):
    return together([values], before)[0]


def exchange(values, expert_count):
    split = values.reshape(expert_count, -1, values.shape[1])
    swapped = lax.all_to_all(split, "expert", split_axis=0, concat_axis=0, tiled=True)
    return swapped.reshape(values.shape)


def swap(values, axis, bit):
    count = lax.axis_size(axis)
    return lax.ppermute(values, axis, [(i, i ^ (1 << bit)) for i in range(count)])


def bits_of(axis):
    return range(lax.axis_size(axis).bit_length() - 1)


def sum_replicas(pair, fill=()):
    bits = list(bits_of("dp"))
    for n in range(len(bits)):
        pair = together(pair)
        others = [swap(pair[0], "dp", bits[n]), swap(pair[1], "dp", bits[-1 - n])]
        if n == len(bits) - 1 and fill:
            others[0] = behind(others[0], *fill)
        pair = [(v.astype(full_type) + o.astype(full_type)).astype(v.dtype) for v, o in zip(pair, others)]
    return pair


def send_blocks(values, *before):
    split = behind(values, *before).reshape(lax.axis_size("expert"), -1, values.shape[1])
    return lax.all_to_all(split, "expert", split_axis=0, concat_axis=0, tiled=True)


def sum_blocks(parts):
    return jnp.sum(parts.astype(full_type), axis=0).astype(parts.dtype)


def scatter_step(values, low, radix, *before):
    place = lax.axis_index("expert")
    split = values.reshape(values.shape[0] // radix, radix, *values.shape[1:])
    own = (place >> low) & (radix - 1)
    terms = []
    for step in range(radix):
        part = lax.dynamic_slice_in_dim(split, own ^ step, 1, 1)[:, 0]
        if step:
            part = lax.ppermute(part, "expert", [(i, i ^ (step << low)) for i in range(lax.axis_size("expert"))])
        elif before:
            part = behind(part, *before)
        terms.append(part.astype(full_type))
    return functools.reduce(jnp.add, terms).astype(values.dtype)


def scatter_chips(values, *before):
    low = 1
    while values.shape[0] > 1:
        radix = min(4, values.shape[0])
        values = scatter_step(values, low, radix, *before)
        low += radix.bit_length() - 1
        before = ()
    return values[0]


def gather_chips(pair, fill=()):
    place = lax.axis_index("expert")
    bits = list(bits_of("expert"))[1:]
    shapes = [v.shape for v in pair]
    pair = [v.reshape((1,) * len(bits) + v.shape) for v in pair]
    for n in range(len(bits)):
        pair = together(pair)
        steps = [bits[n], bits[-1 - n]]
        others = [swap(v, "expert", bit) for v, bit in zip(pair, steps)]
        if n == len(bits) - 1 and fill:
            others[0] = behind(others[0], *fill)
        for k, bit in enumerate(steps):
            axis = len(bits) - bit
            both = [pair[k], others[k]]
            lower, upper = (jnp.concatenate(both[::d], axis=axis) for d in (1, -1))
            pair[k] = jnp.where((place >> bit) & 1 == 0, lower, upper)
    return [v.reshape(-1, *shape) for v, shape in zip(pair, shapes)]


def assemble_body(core_ref, early_ref, early_other_ref, late_ref, late_other_ref, out_ref, query_ref, key_ref, value_ref, small_ref):
    own = pl.program_id(0) % 2 == core_ref[0]
    feat = out_ref.shape[2]
    width = feat // HEAD_GROUPS
    early = jnp.where(own, early_ref[0].astype(full_type), early_other_ref[0].astype(full_type))
    late = jnp.where(own, late_ref[0].astype(full_type), late_other_ref[0].astype(full_type))
    out_ref[0] = early[:, :feat]
    for kind, ref in enumerate((query_ref, key_ref, value_ref)):
        start = kind * width
        ref[0, :, :width] = early[:, feat + start : feat + start + width]
        ref[0, :, width:] = late[:, start : start + width]
    small_ref[0] = late[:, 3 * width :]


def assemble(core, early, early_other, late, late_other):
    chips, rows, early_width = early.shape
    late_width = late.shape[2]
    feat = 2 * chips * rows
    part = lambda width: pl.BlockSpec((1, rows, width), lambda i: (i // 2, 0, 0))
    block = lambda width: pl.BlockSpec((1, rows, width), lambda i: (i, 0, 0))
    matrix, small = out((2 * chips, rows, feat), full_type), out((2 * chips, rows, LANES), full_type)
    results = call(
        assemble_body,
        (matrix,) * 4 + (small,),
        "assemble",
        grid=(2 * chips,),
        in_specs=[pl.BlockSpec(memory_space=pltpu.SMEM)] + [part(early_width)] * 2 + [part(late_width)] * 2,
        out_specs=[block(feat)] * 4 + [block(LANES)],
    )(core, early, early_other, late, late_other)
    return [a.reshape(feat, a.shape[2]) for a in results]


def widen_body(steps, sum_ref, up_ref, down_ref, up_bias_ref, down_bias_ref):
    share, feat = up_ref.shape[0], sum_ref.shape[1]
    for step in range(steps):
        up_ref[:, step * feat : step * feat + feat] = sum_ref[step * share : step * share + share, :].astype(full_type)
    ends = 2 * steps * share
    down_ref[...] = sum_ref[steps * share : ends, :].astype(full_type)
    last = sum_ref[ends:, :].astype(full_type)
    up_bias_ref[...] = last[0:1, : steps * share]
    down_bias_ref[...] = last[8:9, :share]


def widen(expert_sum, steps, share):
    feat = expert_sum.shape[1]
    return call(
        functools.partial(widen_body, steps),
        (
            out((share, steps * feat), full_type),
            out((steps * share, feat), full_type),
            out((1, steps * share), full_type),
            out((1, share), full_type),
        ),
        "widen",
    )(expert_sum)


def shards(
    tokens,
    first_gain,
    first_shift,
    query_weight,
    query_bias,
    key_weight,
    value_weight,
    value_bias,
    out_weight,
    out_bias,
    second_gain,
    second_shift,
    router,
    expert_up,
    expert_up_bias,
    expert_down,
    expert_down_bias,
    choices,
    priority,
    cotangent,
):
    tok_count, feat = tokens.shape
    expert_count = lax.axis_size("expert")
    capacity = (21 * tok_count + 80 * expert_count - 1) // (80 * expert_count) * 8
    router3 = jnp.pad(jnp.concatenate([router] * 3, axis=1), ((0, 0), (0, LANES - 3 * expert_count)))
    up, down = expert_up[0], expert_down[0]

    replicas = lax.axis_size("dp")
    choice_rows = choices.T
    place, cot_sent = route(choice_rows, priority, cotangent, expert_count, capacity)
    cot = exchange(cot_sent, expert_count)
    first, q, k, v, log_big, log_small, attended, middle, _, probs, sent = front(
        tokens,
        (first_gain, first_shift, query_bias, value_bias, out_bias, second_gain, second_shift),
        (query_weight, key_weight, value_weight, out_weight),
        router3,
        place,
        expert_count,
        capacity,
    )
    rows = exchange(behind(sent, cot), expert_count)
    grad_act, start = act_grad(cot, down, expert_down_bias)
    slot = slot_columns(choice_rows, place, capacity, (start,))
    act, grad_pre, gate, score, weight_part = expert(
        rows, up, expert_up_bias, grad_act, start, cot, replicas
    )
    expert_sum = lax.psum_scatter(weight_part, "dp", scatter_dimension=0, tiled=True)[0]
    grad_in = expert_grad_in(grad_pre, up, gate, score, capacity, (slot,))
    back = exchange(grad_in, expert_count)
    result = expert_result(act, down, expert_down_bias, (grad_in,))
    grad_middle, grad_attended, wo_grad, router_part, second_parts = combine(
        back,
        slot,
        probs,
        middle,
        cotangent,
        attended,
        out_weight,
        router3,
        second_gain,
        second_shift,
        expert_count,
        capacity,
        (result,),
    )
    out_blocks = send_blocks(wo_grad, back)
    grads, bias_parts, group_parts, before = [], [], [], ()
    for group in range(HEAD_GROUPS):
        dq, dk, dv, group_part, bias_part = attention_grad(
            group, q, k, v, grad_attended, log_big, log_small, first, before
        )
        grads += [dq, dk, dv]
        bias_parts.append(bias_part)
        group_parts.append(group_part)
        before = (dv, out_blocks)
    first_blocks = send_blocks(group_parts[0], out_blocks)
    token_grad, last_part = input_grad(
        grads,
        query_weight,
        key_weight,
        value_weight,
        tokens,
        first_gain,
        grad_middle,
        bias_parts,
        second_parts,
        router_part,
        group_parts[1],
        (),
    )
    late = behind(last_part, first_blocks).reshape(expert_count, -1, last_part.shape[1])
    late = scatter_chips(scatter_step(late, 0, 2))
    early = jnp.concatenate([sum_blocks(out_blocks), sum_blocks(first_blocks)], axis=1)
    returned = exchange(behind(result, late), expert_count)
    share, steps = feat // replicas, up.shape[1] // feat
    up_grad, down_grad, up_bias_grad, down_bias_grad = widen(expert_sum, steps, share)
    block_output = block_result(returned, slot, probs, middle, expert_count, (token_grad,))
    early, late = gather_chips(sum_replicas([early, late], (up_grad,)), (block_output,))
    early, late = together([early, late])
    core = (lax.axis_index("expert") & 1).reshape(1)
    out_grad, query_grad, key_grad, value_grad, small = assemble(
        core, early, swap(early, "expert", 0), late, swap(late, "expert", 0)
    )
    vectors = small[:, 32:40].T
    return (
        block_output,
        token_grad,
        vectors[0],
        vectors[1],
        query_grad,
        vectors[2],
        key_grad,
        value_grad,
        vectors[3],
        out_grad,
        vectors[6],
        vectors[4],
        vectors[5],
        small[:, :expert_count],
        up_grad[None],
        up_bias_grad,
        down_grad[None],
        down_bias_grad,
    )


def solution(mesh):
    tokens_spec = P(("dp", "expert"), None)
    return jax.shard_map(
        shards,
        mesh=mesh,
        in_specs=(tokens_spec,)
        + (P(),) * 12
        + (P("expert", None, None), P("expert", None), P("expert", None, None), P("expert", None))
        + (tokens_spec,) * 3,
        out_specs=(tokens_spec,) * 2
        + (P(),) * 12
        + (P("expert", "dp", None), P("expert", "dp"), P("expert", "dp", None), P("expert", "dp")),
        check_vma=False,
    )
```

profile of v0, /device:TPU:0, one launch (start us, length us, event | category | flops | bytes accessed | tf_op | source)
XLA Modules:
  0.0 423.6 jit_solution(10982047309400150105)
XLA Ops:
  7.2 7.3 %route.1 = (s32[32,968]{1,0:T(8,128)}, bf16[2048,768]{1,0:T(8,128)(2,1)}) custom-call(s32[2,968]{1,0:T(2,128)} %bitcast.64, s32[1,968]{1,0:T(1,128)} %refs_1_.2, bf16[968,768]{1,0:T(8,128)(2,1)} %refs_4_.3), custom_call_target="tpu_custom_call" | custom-call | flops 1024 | bytes 1024 | tf_op jit(solution)/shard_map/route/pallas_call | solution.py:85
  14.5 5.3 %all-to-all-start = ((bf16[8,256,768]{2,1,0:T(8,128)(2,1)}), bf16[8,256,768]{2,1,0:T(8,128)(2,1)S(1)}, u32[]{:S(2)}, u32[]{:S(2)}) async-start(bf16[8,256,768]{2,1,0:T(8,128)(2,1)} %bitcast.59), calls=%async_computation | async-start | bytes 6291456 | tf_op jit(solution)/shard_map/all_to_all | solution.py:795
  20.7 31.2 %front.1 = (bf16[968,768]{1,0:T(8,128)(2,1)}, bf16[968,768]{1,0:T(8,128)(2,1)}, bf16[968,768]{1,0:T(8,128)(2,1)}, bf16[968,768]{1,0:T(8,128)(2,1)}, f32[12,576]{...) custom-call(bf16[968,768]{1,0:T(8,128)(2,1)} %refs_9_.5, ...), custom_call_target="tpu_custom_call" | custom-call | flops 1024 | bytes 1024 | tf_op jit(solution)/shard_map/front/pallas_call | solution.py:85
  51.9 5.8 %all-to-all-done = bf16[8,256,768]{2,1,0:T(8,128)(2,1)S(1)} async-done(((bf16[8,256,768]{2,1,0:T(8,128)(2,1)}), bf16[8,256,768]{2,1,0:T(8,128)(2,1)S(1)}, u32[]{:S(2)}, u32[]{:S(2)}) %all-to-all-start) | async-done | bytes 3145760 | tf_op jit(solution)/shard_map/all_to_all | solution.py:795
  57.7 1.7 copy-done
  59.4 3.7 all-to-all-start.1
  63.1 19.0 %act_grad.1 = (bf16[2048,3072]{1,0:T(8,128)(2,1)}, f32[2048,128]{1,0:T(8,128)}) custom-call(bf16[2048,768]{1,0:T(8,128)(2,1)} %bitcast.41, bf16[3072,768]{1,0:T(8,128)(2,1)} %bitcast.45, f32[1,768]{1,0:T(1,128)} %refs_2_.9), custom_call_target="tpu_custom_call" | custom-call | flops 1024 | bytes 1024 | tf_op jit(solution)/shard_map/act_grad/pallas_call | solution.py:85
  82.2 2.0 slot_columns.1.refs_4_.refs_1_
  84.1 18.8 %all-to-all-done.1 = bf16[8,272,768]{2,1,0:T(8,128)(2,1)S(1)} async-done(((bf16[8,272,768]{2,1,0:T(8,128)(2,1)}), bf16[8,272,768]{2,1,0:T(8,128)(2,1)S(1)}, u32[]{:S(2)}, u32[]{:S(2)}) %all-to-all-start.1) | async-done | bytes 3342368 | tf_op jit(solution)/shard_map/all_to_all | solution.py:795
  103.0 1.7 copy-done.7
  104.7 53.7 %expert.1 = (bf16[2048,3072]{1,0:T(8,128)(2,1)}, bf16[2048,3072]{1,0:T(8,128)(2,1)}, f32[2048,128]{1,0:T(8,128)}, f32[2048,128]{1,0:T(8,128)}, bf16[4,1552,768]{2,1,0:T(8,128)(2,1)}) custom-call(bf16[2176,768]{1,0:T(8,128)(2,1)} %bitcast.49, bf16[768,3072]{1,0:T(8,128)(2,1)} %bitcast.57, f32[1,3072]{1,0:T(1,128)} %refs_2_.8, ...), custom_call_target="tpu_custom_call" | custom-call | flops 1024 | bytes 1024 | tf_op jit(solution)/shard_map/expert/pallas_call | solution.py:85
  158.4 15.7 %grad_in.1.refs_3_ = bf16[2176,768]{1,0:T(8,128)(2,1)} custom-call(bf16[2048,3072]{1,0:T(8,128)(2,1)} %get-tuple-element.79.refs_0_, bf16[768,3072]{1,0:T(8,128)(2,1)} %bitcast.58, f32[2048,128]{1,0:T(8,128)} %get-tuple-element.80.refs_2_, f32[2048,128]{1,0:T(8,128)} %get-tuple-element.81.refs_3_, s32[968,2]{1,0:T(8,128)} %slot_columns.1.refs_4_.refs_1_), custom_call_target="tpu_custom_call" | custom-call | flops 399999991808 | bytes 1024 | tf_op jit(solution)/shard_map/grad_in/pallas_call | solution.py:85
  174.2 3.7 all-to-all-start.2
  177.8 14.8 %result.1.refs_10_.refs_0_ = bf16[2048,768]{1,0:T(8,128)(2,1)} custom-call(bf16[2048,3072]{1,0:T(8,128)(2,1)} %get-tuple-element.78.refs_0_, bf16[3072,768]{1,0:T(8,128)(2,1)} %bitcast.46, f32[1,768]{1,0:T(1,128)} %refs_2_.9, bf16[2176,768]{1,0:T(8,128)(2,1)} %grad_in.1.refs_3_), custom_call_target="tpu_custom_call" | custom-call | flops 1024 | bytes 1024 | tf_op jit(solution)/shard_map/result/pallas_call | solution.py:85
  192.6 25.1 %all-to-all-done.2 = bf16[8,272,768]{2,1,0:T(8,128)(2,1)S(1)} async-done(((bf16[8,272,768]{2,1,0:T(8,128)(2,1)}), bf16[8,272,768]{2,1,0:T(8,128)(2,1)S(1)}, u32[]{:S(2)}, u32[]{:S(2)}) %all-to-all-start.2) | async-done | bytes 3342368 | tf_op jit(solution)/shard_map/all_to_all | solution.py:795
  217.7 1.7 copy-done.1
  219.5 17.7 %combine.1 = (f32[968,768]{1,0:T(8,128)}, bf16[968,768]{1,0:T(8,128)(2,1)}, bf16[768,768]{1,0:T(8,128)(2,1)}, f32[768,128]{1,0:T(8,128)}, f32[3,768]{1,0:T(4,128)}) custom-call(bf16[2176,768]{1,0:T(8,128)(2,1)} %bitcast.43, s32[968,2]{1,0:T(8,128)} %slot_columns.1.refs_4_.refs_1_, f32[968,128]{1,0:T(8,128)} %get-tuple-element.85.refs_2_, ...), custom_call_target="tpu_custom_call" | custom-call | flops 1024 | bytes 1024 | tf_op jit(solution)/shard_map/combine/pallas_call | solution.py:85
  237.1 4.0 all-to-all-start.3
  241.1 17.4 %attention_grad_0.1 = (bf16[968,384]{1,0:T(8,128)(2,1)}, bf16[968,384]{1,0:T(8,128)(2,1)}, bf16[968,384]{1,0:T(8,128)(2,1)}, bf16[768,1152]{1,0:T(8,128)(2,1)}, f32[2,384]{1,0:T(2,128)}) custom-call(bf16[968,768]{1,0:T(8,128)(2,1)} %get-tuple-element.82.refs_0_, bf16[968,768]{1,0:T(8,128)(2,1)} %get-tuple-element.83.refs_1_, ...), custom_call_target="tpu_custom_call" | custom-call | flops 1024 | bytes 1024 | tf_op jit(solution)/shard_map/attention_grad_0/pallas_call | solution.py:85
  258.5 1.0 copy-done.2
  259.5 4.2 all-to-all-start.4
  263.7 17.5 %attention_grad_1.1 = (bf16[968,384]{1,0:T(8,128)(2,1)}, bf16[968,384]{1,0:T(8,128)(2,1)}, bf16[968,384]{1,0:T(8,128)(2,1)}, bf16[768,1280]{1,0:T(8,128)(2,1)}, f32[2,384]{1,0:T(2,128)}) custom-call(bf16[968,768]{1,0:T(8,128)(2,1)} %get-tuple-element.82.refs_0_, bf16[968,768]{1,0:T(8,128)(2,1)} %get-tuple-element.83.refs_1_, ...), custom_call_target="tpu_custom_call" | custom-call | flops 1024 | bytes 1024 | tf_op jit(solution)/shard_map/attention_grad_1/pallas_call | solution.py:85
  281.1 11.6 %input_grad.1 = (bf16[968,768]{1,0:T(8,128)(2,1)}, bf16[768,1280]{1,0:T(8,128)(2,1)}) custom-call(bf16[968,384]{1,0:T(8,128)(2,1)} %get-tuple-element.92.refs_0_, bf16[968,384]{1,0:T(8,128)(2,1)} %get-tuple-element.93.refs_1_, bf16[968,384]{1,0:T(8,128)(2,1)} %get-tuple-element.94.refs_7_.refs_2_, ...), custom_call_target="tpu_custom_call", output_to_operand_aliasing={{1}: (16, {})} | custom-call | flops 1024 | bytes 1024 | tf_op jit(solution)/shard_map/input_grad/pallas_call | solution.py:85
  292.7 1.2 copy-done.5
  293.9 2.4 dynamic-slice_bitcast_fusion
  296.8 2.5 collective-permute-done
  299.3 1.4 fusion
  300.8 0.9 copy-done.11
  301.7 0.8 constant_dynamic-slice_fusion.2
  302.5 1.9 collective-permute-start.1
  304.4 1.5 collective-permute-start.2
  306.5 5.2 %collective-permute-done.1 = bf16[1,96,1280]{2,1,0:T(8,128)(2,1)} collective-permute-done((bf16[1,96,1280]{2,1,0:T(8,128)(2,1)}, bf16[1,96,1280]{2,1,0:T(8,128)(2,1)}, u32[]{:S(2)}, u32[]{:S(2)}) %collective-permute-start.1) | collective-permute-done | bytes 245792 | tf_op jit(solution)/shard_map/ppermute | solution.py:836
  311.6 6.1 %collective-permute-done.2 = bf16[1,96,1280]{2,1,0:T(8,128)(2,1)} collective-permute-done((bf16[1,96,1280]{2,1,0:T(8,128)(2,1)}, bf16[1,96,1280]{2,1,0:T(8,128)(2,1)}, u32[]{:S(2)}, u32[]{:S(2)}) %collective-permute-start.2) | collective-permute-done | bytes 245792 | tf_op jit(solution)/shard_map/ppermute | solution.py:836
  317.7 2.1 fusion.2.refs_1_
  319.8 0.8 pad_maximum_fusion.refs_0_
  320.6 2.7 collective-permute-start.5
  323.3 1.6 collective-permute-start.4
  324.9 4.0 all-to-all-start.5
  328.9 5.3 %collective-permute-done.5 = bf16[96,1280]{1,0:T(8,128)(2,1)} collective-permute-done((bf16[96,1280]{1,0:T(8,128)(2,1)}, bf16[96,1280]{1,0:T(8,128)(2,1)}, u32[]{:S(2)}, u32[]{:S(2)}) %collective-permute-start.5) | collective-permute-done | bytes 245792 | tf_op jit(solution)/shard_map/ppermute | solution.py:801
  334.2 1.7 add_convert_fusion.3.refs_1_
  335.9 1.0 collective-permute-done.4
  336.9 1.9 add_convert_fusion.1.refs_0_
  338.8 1.6 collective-permute-start.7
  340.5 1.7 collective-permute-start.6
  342.2 8.1 %collective-permute-done.7 = bf16[96,1280]{1,0:T(8,128)(2,1)S(1)} collective-permute-done((bf16[96,1280]{1,0:T(8,128)(2,1)}, bf16[96,1280]{1,0:T(8,128)(2,1)S(1)}, u32[]{:S(2)}, u32[]{:S(2)}) %collective-permute-start.7) | collective-permute-done | bytes 245792 | tf_op jit(solution)/shard_map/ppermute | solution.py:801
  350.3 1.7 fusion.3.refs_1_
  352.0 4.0 widen.1
  356.0 2.6 collective-permute-done.6.refs_0_
  358.6 1.8 fusion.1.refs_0_
  360.5 1.4 collective-permute-start.9
  362.5 9.6 %collective-permute-done.9 = bf16[1,1,96,1280]{3,2,1,0:T(8,128)(2,1)} collective-permute-done((bf16[1,1,96,1280]{3,2,1,0:T(8,128)(2,1)}, bf16[1,1,96,1280]{3,2,1,0:T(8,128)(2,1)}, u32[]{:S(2)}, u32[]{:S(2)}) %collective-permute-start.9) | collective-permute-done | bytes 245792 | tf_op jit(solution)/shard_map/ppermute | solution.py:801
  372.1 2.2 maximum_select_fusion.3.refs_1_
  374.2 2.1 maximum_select_fusion.2.refs_0_
  376.8 1.0 collective-permute-start.10
  377.8 1.6 copy-done.8
  379.5 11.4 %block_result.1.refs_1_ = bf16[968,768]{1,0:T(8,128)(2,1)} custom-call(bf16[2048,768]{1,0:T(8,128)(2,1)} %bitcast.53, s32[968,2]{1,0:T(8,128)} %slot_columns.1.refs_4_.refs_1_, f32[968,128]{1,0:T(8,128)} %get-tuple-element.85.refs_2_, f32[968,768]{1,0:T(8,128)} %get-tuple-element.86.refs_3_, bf16[968,768]{1,0:T(8,128)(2,1)} %get-tuple-element.56.refs_4_), custom_call_target="tpu_custom_call" | custom-call | flops 1024 | bytes 1024 | tf_op jit(solution)/shard_map/block_result/pallas_call | solution.py:85
  390.9 2.3 maximum_select_fusion.1
  393.2 2.1 collective-permute-done.10.refs_0_
  395.3 2.7 maximum_select_fusion
  398.6 4.4 %collective-permute-done.13.refs_4_ = bf16[4,96,1280]{2,1,0:T(8,128)(2,1)S(1)} collective-permute-done((bf16[4,96,1280]{2,1,0:T(8,128)(2,1)}, bf16[4,96,1280]{2,1,0:T(8,128)(2,1)S(1)}, u32[]{:S(2)}, u32[]{:S(2)}) %collective-permute-start.13) | collective-permute-done | bytes 983072 | tf_op jit(solution)/shard_map/ppermute | solution.py:801
  403.0 0.9 copy-done.15
  404.4 9.3 %assemble.1 = (f32[8,96,768]{2,1,0:T(8,128)}, f32[8,96,768]{2,1,0:T(8,128)}, f32[8,96,768]{2,1,0:T(8,128)}, f32[8,96,768]{2,1,0:T(8,128)}, f32[8,96,128]{2,1,0:T(8,128)}) custom-call(s32[1]{0:T(128)} %bitcast.17.refs_0_, bf16[4,96,1920]{2,1,0:T(8,128)(2,1)} %get-tuple-element.118.refs_1_, bf16[4,96,1920]{2,1,0:T(8,128)(2,1)} %copy-done.14, ...), custom_call_target="tpu_custom_call" | custom-call | flops 1024 | bytes 1024 | tf_op jit(solution)/shard_map/assemble/pallas_call | solution.py:85
  413.7 1.3 fusion.4
  415.8 0.7 copy.72
  (61 shorter events, 5.0 us)
Async XLA Ops:
  14.5 5.3 %copy-start.16 = (bf16[768,8]{0,1:T(8,128)(2,1)S(1)}, bf16[768,8]{0,1:T(8,128)(2,1)}, u32[]{:S(2)}) copy-start(bf16[768,8]{0,1:T(8,128)(2,1)} %param.32) | copy-start | bytes 36868
  14.5 43.2 %all-to-all-start = ((bf16[8,256,768]{2,1,0:T(8,128)(2,1)}), bf16[8,256,768]{2,1,0:T(8,128)(2,1)S(1)}, u32[]{:S(2)}, u32[]{:S(2)}) async-start(bf16[8,256,768]{2,1,0:T(8,128)(2,1)} %bitcast.59), calls=%async_computation | async-start | bytes 6291456 | tf_op jit(solution)/shard_map/all_to_all | solution.py:795
  57.7 1.7 copy-start
  59.4 43.6 %all-to-all-start.1 = ((bf16[8,272,768]{2,1,0:T(8,128)(2,1)}), bf16[8,272,768]{2,1,0:T(8,128)(2,1)S(1)}, u32[]{:S(2)}, u32[]{:S(2)}) async-start(bf16[8,272,768]{2,1,0:T(8,128)(2,1)} %bitcast.51), calls=%async_computation.1 | async-start | bytes 6684672 | tf_op jit(solution)/shard_map/all_to_all | solution.py:795
  63.1 288.9 %reduce-scatter.2.cloned.1.call-start = ((), (), s32[]{:S(2)}) async-start(), calls=%async_computation.7 | async-start | bytes 11919360 | tf_op jit(solution)/shard_map/reduce_scatter | solution.py:976
  103.0 1.7 copy-start.7
  174.2 43.6 %all-to-all-start.2 = ((bf16[8,272,768]{2,1,0:T(8,128)(2,1)}), bf16[8,272,768]{2,1,0:T(8,128)(2,1)S(1)}, u32[]{:S(2)}, u32[]{:S(2)}) async-start(bf16[8,272,768]{2,1,0:T(8,128)(2,1)} %bitcast.50), calls=%async_computation.2 | async-start | bytes 6684672 | tf_op jit(solution)/shard_map/all_to_all | solution.py:795
  217.7 1.7 copy-start.1
  237.1 21.4 %all-to-all-start.3 = ((bf16[8,96,768]{2,1,0:T(8,128)(2,1)}), bf16[8,96,768]{2,1,0:T(8,128)(2,1)S(1)}, u32[]{:S(2)}, u32[]{:S(2)}) async-start(bf16[8,96,768]{2,1,0:T(8,128)(2,1)} %bitcast.56), calls=%async_computation.3 | async-start | bytes 2359296 | tf_op jit(solution)/shard_map/all_to_all | solution.py:821
  258.5 1.0 copy-start.2
  259.5 33.2 %all-to-all-start.4 = ((bf16[8,96,1152]{2,1,0:T(8,128)(2,1)}), bf16[8,96,1152]{2,1,0:T(8,128)(2,1)S(1)}, u32[]{:S(2)}, u32[]{:S(2)}) async-start(bf16[8,96,1152]{2,1,0:T(8,128)(2,1)} %bitcast.55), calls=%async_computation.4 | async-start | bytes 3538944 | tf_op jit(solution)/shard_map/all_to_all | solution.py:821
  292.7 1.2 copy-start.5
  293.9 5.4 %copy-start.4 = (bf16[768,1280]{1,0:T(8,128)(2,1)S(1)}, bf16[768,1280]{1,0:T(8,128)(2,1)}, u32[]{:S(2)}) copy-start(bf16[768,1280]{1,0:T(8,128)(2,1)} %together.15) | copy-start | bytes 5898244
  296.3 3.0 collective-permute-start
  296.8 9.2 %copy-start.3 = (bf16[8,96,768]{2,1,0:T(8,128)(2,1)S(1)}, bf16[8,96,768]{2,1,0:T(8,128)(2,1)}, u32[]{:S(2)}) copy-start(bf16[8,96,768]{2,1,0:T(8,128)(2,1)} %copy-done.2) | copy-start | bytes 3538948
  300.8 0.9 copy-start.11
  301.7 4.5 %copy-start.6 = (bf16[8,96,1152]{2,1,0:T(8,128)(2,1)S(1)}, bf16[8,96,1152]{2,1,0:T(8,128)(2,1)}, u32[]{:S(2)}) copy-start(bf16[8,96,1152]{2,1,0:T(8,128)(2,1)} %copy-done.5) | copy-start | bytes 5308420
  302.5 9.1 %collective-permute-start.1 = (bf16[1,96,1280]{2,1,0:T(8,128)(2,1)}, bf16[1,96,1280]{2,1,0:T(8,128)(2,1)}, u32[]{:S(2)}, u32[]{:S(2)}) collective-permute-start(bf16[1,96,1280]{2,1,0:T(8,128)(2,1)} %get-tuple-element.135), channel_id=1, source_target_pairs={{0,2},{1,3},{2,0},{3,1},{4,6},{5,7},{6,4},{7,5},{8,10},{9,11},{10,... | collective-permute-start | bytes 737288 | tf_op jit(solution)/shard_map/ppermute | solution.py:836
  304.4 13.3 %collective-permute-start.2 = (bf16[1,96,1280]{2,1,0:T(8,128)(2,1)}, bf16[1,96,1280]{2,1,0:T(8,128)(2,1)}, u32[]{:S(2)}, u32[]{:S(2)}) collective-permute-start(bf16[1,96,1280]{2,1,0:T(8,128)(2,1)} %get-tuple-element.137), channel_id=1, source_target_pairs={{0,4},{1,5},{2,6},{3,7},{4,0},{5,1},{6,2},{7,3},{8,12},{9,13},{10,... | collective-permute-start | bytes 737288 | tf_op jit(solution)/shard_map/ppermute | solution.py:836
  305.9 11.8 %collective-permute-start.3 = (bf16[1,96,1280]{2,1,0:T(8,128)(2,1)S(1)}, bf16[1,96,1280]{2,1,0:T(8,128)(2,1)}, u32[]{:S(2)}, u32[]{:S(2)}) collective-permute-start(bf16[1,96,1280]{2,1,0:T(8,128)(2,1)S(1)} %get-tuple-element.136), channel_id=1, source_target_pairs={{0,6},{1,7},{2,4},{3,5},{4,2},{5,3},{6,0},{7,1},{8,14},{9,15},{10,... | collective-permute-start | bytes 737288 | tf_op jit(solution)/shard_map/ppermute | solution.py:836
  320.6 13.6 %collective-permute-start.5 = (bf16[96,1280]{1,0:T(8,128)(2,1)}, bf16[96,1280]{1,0:T(8,128)(2,1)}, u32[]{:S(2)}, u32[]{:S(2)}) collective-permute-start(bf16[96,1280]{1,0:T(8,128)(2,1)} %get-tuple-element.109), channel_id=1, source_target_pairs={{0,16},{8,24},{16,0},{24,8},{1,17},{9,25},{17,1},{25,9},{2,18},{10... | collective-permute-start | bytes 737288 | tf_op jit(solution)/shard_map/ppermute | solution.py:801
  323.3 13.6 %collective-permute-start.4 = (bf16[96,1920]{1,0:T(8,128)(2,1)}, bf16[96,1920]{1,0:T(8,128)(2,1)}, u32[]{:S(2)}, u32[]{:S(2)}) collective-permute-start(bf16[96,1920]{1,0:T(8,128)(2,1)} %get-tuple-element.108), channel_id=1, source_target_pairs={{0,8},{8,0},{16,24},{24,16},{1,9},{9,1},{17,25},{25,17},{2,10},{10... | collective-permute-start | bytes 1105928 | tf_op jit(solution)/shard_map/ppermute | solution.py:801
  324.9 9.3 %copy-start.12 = (bf16[96,1280]{1,0:T(8,128)(2,1)S(1)}, bf16[96,1280]{1,0:T(8,128)(2,1)}, u32[]{:S(2)}) copy-start(bf16[96,1280]{1,0:T(8,128)(2,1)} %get-tuple-element.109) | copy-start | bytes 737284
  324.9 52.9 %all-to-all-start.5 = ((bf16[8,256,768]{2,1,0:T(8,128)(2,1)}), bf16[8,256,768]{2,1,0:T(8,128)(2,1)S(1)}, u32[]{:S(2)}, u32[]{:S(2)}) async-start(bf16[8,256,768]{2,1,0:T(8,128)(2,1)} %bitcast.39), calls=%async_computation.5 | async-start | bytes 6291456 | tf_op jit(solution)/shard_map/all_to_all | solution.py:795
  338.8 11.4 %collective-permute-start.7 = (bf16[96,1280]{1,0:T(8,128)(2,1)}, bf16[96,1280]{1,0:T(8,128)(2,1)S(1)}, u32[]{:S(2)}, u32[]{:S(2)}) collective-permute-start(bf16[96,1280]{1,0:T(8,128)(2,1)} %get-tuple-element.113), channel_id=1, source_target_pairs={{0,8},{8,0},{16,24},{24,16},{1,9},{9,1},{17,25},{25,17},{2,10},{10... | collective-permute-start | bytes 737288 | tf_op jit(solution)/shard_map/ppermute | solution.py:801
  340.5 18.2 %collective-permute-start.6 = (bf16[96,1920]{1,0:T(8,128)(2,1)}, bf16[96,1920]{1,0:T(8,128)(2,1)}, u32[]{:S(2)}, u32[]{:S(2)}) collective-permute-start(bf16[96,1920]{1,0:T(8,128)(2,1)} %get-tuple-element.110), channel_id=1, source_target_pairs={{0,16},{8,24},{16,0},{24,8},{1,17},{9,25},{17,1},{25,9},{2,18},{10... | collective-permute-start | bytes 1105928 | tf_op jit(solution)/shard_map/ppermute | solution.py:801
  356.0 2.6 copy-start.13
  360.5 11.6 %collective-permute-start.9 = (bf16[1,1,96,1280]{3,2,1,0:T(8,128)(2,1)}, bf16[1,1,96,1280]{3,2,1,0:T(8,128)(2,1)}, u32[]{:S(2)}, u32[]{:S(2)}) collective-permute-start(bf16[1,1,96,1280]{3,2,1,0:T(8,128)(2,1)} %get-tuple-element.115), channel_id=1, source_target_pairs={{0,4},{1,5},{2,6},{3,7},{4,0},{5,1},{6,2},{7,3},{8,12},{9,13},{10,... | collective-permute-start | bytes 737288 | tf_op jit(solution)/shard_map/ppermute | solution.py:801
  361.8 12.4 %collective-permute-start.8 = (bf16[1,1,96,1920]{3,2,1,0:T(8,128)(2,1)}, bf16[1,1,96,1920]{3,2,1,0:T(8,128)(2,1)S(1)}, u32[]{:S(2)}, u32[]{:S(2)}) collective-permute-start(bf16[1,1,96,1920]{3,2,1,0:T(8,128)(2,1)} %get-tuple-element.114), channel_id=1, source_target_pairs={{0,2},{1,3},{2,0},{3,1},{4,6},{5,7},{6,4},{7,5},{8,10},{9,11},{10,... | collective-permute-start | bytes 1105928 | tf_op jit(solution)/shard_map/ppermute | solution.py:801
  376.3 14.6 %collective-permute-start.11 = (bf16[2,1,96,1280]{3,2,1,0:T(8,128)(2,1)}, bf16[2,1,96,1280]{3,2,1,0:T(8,128)(2,1)}, u32[]{:S(2)}, u32[]{:S(2)}) collective-permute-start(bf16[2,1,96,1280]{3,2,1,0:T(8,128)(2,1)} %get-tuple-element.117), channel_id=1, source_target_pairs={{0,2},{1,3},{2,0},{3,1},{4,6},{5,7},{6,4},{7,5},{8,10},{9,11},{10,... | collective-permute-start | bytes 1474568 | tf_op jit(solution)/shard_map/ppermute | solution.py:801
  376.8 18.5 %collective-permute-start.10 = (bf16[1,2,96,1920]{3,2,1,0:T(8,128)(2,1)}, bf16[1,2,96,1920]{3,2,1,0:T(8,128)(2,1)}, u32[]{:S(2)}, u32[]{:S(2)}) collective-permute-start(bf16[1,2,96,1920]{3,2,1,0:T(8,128)(2,1)} %get-tuple-element.116), channel_id=1, source_target_pairs={{0,4},{1,5},{2,6},{3,7},{4,0},{5,1},{6,2},{7,3},{8,12},{9,13},{10,... | collective-permute-start | bytes 2211848 | tf_op jit(solution)/shard_map/ppermute | solution.py:801
  377.8 1.6 copy-start.8
  379.5 11.4 %copy-start.10 = (bf16[2,1,96,1280]{3,2,1,0:T(8,128)(2,1)S(1)}, bf16[2,1,96,1280]{3,2,1,0:T(8,128)(2,1)}, u32[]{:S(2)}) copy-start(bf16[2,1,96,1280]{3,2,1,0:T(8,128)(2,1)} %get-tuple-element.117) | copy-start | bytes 1474564
  393.2 2.1 copy-start.9
  398.1 4.9 %collective-permute-start.12 = (bf16[4,96,1920]{2,1,0:T(8,128)(2,1)}, bf16[4,96,1920]{2,1,0:T(8,128)(2,1)S(1)}, u32[]{:S(2)}, u32[]{:S(2)}) collective-permute-start(bf16[4,96,1920]{2,1,0:T(8,128)(2,1)} %get-tuple-element.118.refs_1_), channel_id=1, source_target_pairs={{0,1},{1,0},{2,3},{3,2},{4,5},{5,4},{6,7},{7,6},{8,9},{9,8},{10,11... | collective-permute-start | bytes 4423688 | tf_op jit(solution)/shard_map/ppermute | solution.py:801
  398.1 4.9 %collective-permute-start.13 = (bf16[4,96,1280]{2,1,0:T(8,128)(2,1)}, bf16[4,96,1280]{2,1,0:T(8,128)(2,1)S(1)}, u32[]{:S(2)}, u32[]{:S(2)}) collective-permute-start(bf16[4,96,1280]{2,1,0:T(8,128)(2,1)} %get-tuple-element.119.refs_3_), channel_id=1, source_target_pairs={{0,1},{1,0},{2,3},{3,2},{4,5},{5,4},{6,7},{7,6},{8,9},{9,8},{10,11... | collective-permute-start | bytes 2949128 | tf_op jit(solution)/shard_map/ppermute | solution.py:801
  402.9 1.0 copy-start.15
  403.0 1.5 copy-start.14
Sparse Core Ops, SparseCore 0:
  158.6 162.6 reduce-scatter.1
where the time goes:
time: 432 us; the launch traced here: 424 us
  Pallas kernels  233 us (54%)
  waiting for transfers between devices  96.7 us (22%)
  starting transfers between devices  40.4 us (9%)
  other arithmetic  21.2 us (5%)
  local copies, waits for them, and re-layouts  18.3 us (4%)
  between operations  14.4 us (3%)
    pallas_call x14, Pallas kernels, build(): pl.pallas_call(inner, out_shape=out_shape, name=name, grid=grid, in_specs...  233 us
    all_to_all x4, waiting for transfers between devices, exchange(): lax.all_to_all(split, 'expert', split_axis=0, concat_axis=0, tiled=True)  49.7 us
    ppermute x10, waiting for transfers between devices, swap(): return lax.ppermute(values, axis, [(i, i ^ 1 << bit) for i in range(count)])  33.1 us
    all_to_all x4, starting transfers between devices, exchange(): lax.all_to_all(split, 'expert', split_axis=0, concat_axis=0, tiled=True)  16.6 us
    ppermute x4, waiting for transfers between devices, scatter_step(): lax.ppermute(part, 'expert', [(i, i ^ step << low) for i in range(lax.axi...  13.8 us
    unnamed x36, local copies, waits for them, and re-layouts  12.3 us
    ppermute x10, starting transfers between devices, swap(): return lax.ppermute(values, axis, [(i, i ^ 1 << bit) for i in range(count)])  11.7 us
    select_n x4, other arithmetic, gather_chips(): pair[k] = jnp.where(place >> bit & 1 == 0, lower, upper)  9.28 us
  transfers between devices with their start and end apart: 21, of which 13 were waited for; matrix products, arithmetic and copies ran while one was open for 5% of the time, Pallas kernels for 38%

commit v1 on v0

--- a/solution.py
+++ b/solution.py
@@ -388,7 +388,7 @@
     return values * area, area + values * bell
 
 
-def expert_body(rows_ref, up_ref, up_bias_ref, grad_act_ref, start_ref, cot_ref, act_ref, grad_pre_ref, gate_ref, score_ref, sum_ref, x_ref, gated_ref, grad_ref, bias_ref, up_out_ref, down_out_ref, sems):
+def expert_body(rows_ref, up_ref, up_bias_ref, grad_act_ref, start_ref, cot_ref, act_ref, grad_pre_ref, gate_ref, score_ref, sum_ref, x_ref, gated_ref, grad_ref, bias_ref, up_out_ref, down_out_ref, cot_held, start_held, sems, load_sems):
     slots, feat = cot_ref.shape
     replicas, share = up_out_ref.shape[1:3]
     steps = (sum_ref.shape[1] - EXTRA) // share // 2
@@ -406,24 +406,20 @@
             pairs.append((down_out_ref.at[step % 2, pl.ds(piece * size, size)], target))
         return [pltpu.make_async_copy(a, b, sems.at[step, i]) for i, (a, b) in enumerate(pairs)]
 
+    loads = [
+        pltpu.make_async_copy(cot_ref, cot_held, load_sems.at[0]),
+        pltpu.make_async_copy(start_ref, start_held, load_sems.at[1]),
+    ]
+
     @pl.when(number == 0)
     def _():
-        total = jnp.zeros((1, feat), full_type)
+        for load in loads:
+            load.start()
         for e in range(slots // capacity):
             rows = pl.ds(e * capacity, capacity)
-            gate = thirds_to_lanes(rows_ref[pl.ds(e * part + capacity, EXTRA), 0:capacity])
-            gate_ref[rows, :] = gate
-            wide = jnp.concatenate([gate] * (feat // LANES), axis=1)
-            x = rows_ref[pl.ds(e * part, capacity), :]
-            x_ref[rows, :] = x
-            gated_ref[rows, :] = (x.astype(full_type) * wide).astype(half_type)
-            grad = (cot_ref[rows, :].astype(full_type) * wide).astype(half_type)
-            grad_ref[rows, :] = grad
-            total = total + jnp.sum(grad.astype(full_type), axis=0, keepdims=True)
-        bias_ref[...] = jnp.zeros(bias_ref.shape, half_type)
-        for z in range(replicas):
-            bias_ref[z, 8:9, 0:share] = total[:, z * share : z * share + share].astype(half_type)
-        score_ref[...] = start_ref[...]
+            gate_ref[rows, :] = thirds_to_lanes(rows_ref[pl.ds(e * part + capacity, EXTRA), 0:capacity])
+            x_ref[rows, :] = rows_ref[pl.ds(e * part, capacity), :]
+        score_ref[...] = jnp.zeros(score_ref.shape, full_type)
 
     blocks = row_blocks(slots, 512)
     pre = mul(x_ref[pl.ds(*blocks[0]), :], up_ref[...])
@@ -438,6 +434,22 @@
         score_ref[rows, :] += fold_lanes(act * grad_act)
         grad_pre_ref[rows, :] = (grad_act * slope).astype(half_type)
         pre = later
+    @pl.when(number == 0)
+    def _():
+        for load in loads:
+            load.wait()
+        total = jnp.zeros((1, feat), full_type)
+        for e in range(slots // capacity):
+            rows = pl.ds(e * capacity, capacity)
+            wide = jnp.concatenate([gate_ref[rows, :]] * (feat // LANES), axis=1)
+            gated_ref[rows, :] = (x_ref[rows, :].astype(full_type) * wide).astype(half_type)
+            grad = (cot_held[rows, :].astype(full_type) * wide).astype(half_type)
+            grad_ref[rows, :] = grad
+            total = total + jnp.sum(grad.astype(full_type), axis=0, keepdims=True)
+        bias_ref[...] = jnp.zeros(bias_ref.shape, half_type)
+        for z in range(replicas):
+            bias_ref[z, 8:9, 0:share] = total[:, z * share : z * share + share].astype(half_type)
+
     for step in range(2, steps):
 
         @pl.when(number == step)
@@ -465,7 +477,7 @@
     def _():
         last = pltpu.make_async_copy(bias_ref, sum_ref.at[:, pl.ds(2 * down_rows, EXTRA), :], sems.at[0, 0])
         last.start()
-        score_ref[...] = score_ref[...] * gate_ref[...]
+        score_ref[...] = (score_ref[...] + start_held[...]) * gate_ref[...]
         for step in range(steps - 2, steps):
             for copy in copies(step):
                 copy.wait()
@@ -495,8 +507,8 @@
             pl.BlockSpec((feat, feat), lambda f: (0, f)),
             pl.BlockSpec((1, feat), lambda f: (0, f)),
             wide,
-            once(start),
-            once(cot),
+            pl.BlockSpec(memory_space=pl.ANY),
+            pl.BlockSpec(memory_space=pl.ANY),
         ],
         out_specs=[
             wide,
@@ -512,7 +524,10 @@
             pltpu.VMEM((replicas, EXTRA, feat), half_type),
             pltpu.VMEM((2, replicas, share, feat), half_type),
             pltpu.VMEM((2, feat, feat), half_type),
+            pltpu.VMEM((slots, feat), half_type),
+            pltpu.VMEM((slots, LANES), full_type),
             pltpu.SemaphoreType.DMA((steps, 1 + max(1, feat // (steps * share)))),
+            pltpu.SemaphoreType.DMA((2,)),
         ],
     )(rows, up, up_bias, grad_act, start, cot)
 
@@ -786,6 +801,10 @@
     return list(call_all(*values, *before))
 
 
+def mark(values):
+    return values.reshape(-1, values.shape[-1])[:8, :LANES]
+
+
 def behind(values, *before):
     return together([values], before)[0]
 
@@ -851,7 +870,6 @@
 
 
 def gather_chips(pair, fill=()):
-    place = lax.axis_index("expert")
     bits = list(bits_of("expert"))[1:]
     shapes = [v.shape for v in pair]
     pair = [v.reshape((1,) * len(bits) + v.shape) for v in pair]
@@ -861,44 +879,60 @@
         others = [swap(v, "expert", bit) for v, bit in zip(pair, steps)]
         if n == len(bits) - 1 and fill:
             others[0] = behind(others[0], *fill)
-        for k, bit in enumerate(steps):
-            axis = len(bits) - bit
-            both = [pair[k], others[k]]
-            lower, upper = (jnp.concatenate(both[::d], axis=axis) for d in (1, -1))
-            pair[k] = jnp.where((place >> bit) & 1 == 0, lower, upper)
+        pair = [jnp.concatenate([v, o], axis=len(bits) - bit) for v, o, bit in zip(pair, others, steps)]
     return [v.reshape(-1, *shape) for v, shape in zip(pair, shapes)]
 
 
-def assemble_body(core_ref, early_ref, early_other_ref, late_ref, late_other_ref, out_ref, query_ref, key_ref, value_ref, small_ref):
-    own = pl.program_id(0) % 2 == core_ref[0]
-    feat = out_ref.shape[2]
+def assemble_body(place_ref, early_ref, early_other_ref, late_ref, late_other_ref, *refs):
+    out_ref, query_ref, key_ref, value_ref, router_ref = refs[:5]
+    vector_refs, held_ref = refs[5:-1], refs[-1]
+    rows, feat = out_ref.shape[1:]
     width = feat // HEAD_GROUPS
-    early = jnp.where(own, early_ref[0].astype(full_type), early_other_ref[0].astype(full_type))
-    late = jnp.where(own, late_ref[0].astype(full_type), late_other_ref[0].astype(full_type))
-    out_ref[0] = early[:, :feat]
-    for kind, ref in enumerate((query_ref, key_ref, value_ref)):
-        start = kind * width
-        ref[0, :, :width] = early[:, feat + start : feat + start + width]
-        ref[0, :, width:] = late[:, start : start + width]
-    small_ref[0] = late[:, 3 * width :]
-
-
-def assemble(core, early, early_other, late, late_other):
+    own = lax.rem(place_ref[0], 2)
+    number = pl.program_id(0)
+    for core, early_part, late_part in ((own, early_ref, late_ref), (1 - own, early_other_ref, late_other_ref)):
+        early, late = early_part[0].astype(full_type), late_part[0].astype(full_type)
+        out_ref[core] = early[:, :feat]
+        for kind, ref in enumerate((query_ref, key_ref, value_ref)):
+            start = kind * width
+            moved = feat + start if kind < 2 else 3 * width + LANES
+            ref[core, :, :width] = (early if kind < 2 else late)[:, moved : moved + width]
+            ref[core, :, width:] = late[:, start : start + width]
+        small = late[:, 3 * width : 3 * width + LANES]
+        held_ref[pl.ds(pl.multiple_of((2 * number + core) * rows, 8), rows), :] = small
+
+    @pl.when(number == pl.num_programs(0) - 1)
+    def _():
+        small = held_ref[...]
+        columns = small.T
+        router_ref[...] = columns[: router_ref.shape[0]]
+        for k, ref in enumerate(vector_refs):
+            ref[...] = columns[32 + k]
+
+
+def assemble(place, early, early_other, late, late_other, expert_count):
     chips, rows, early_width = early.shape
     late_width = late.shape[2]
     feat = 2 * chips * rows
-    part = lambda width: pl.BlockSpec((1, rows, width), lambda i: (i // 2, 0, 0))
-    block = lambda width: pl.BlockSpec((1, rows, width), lambda i: (i, 0, 0))
-    matrix, small = out((2 * chips, rows, feat), full_type), out((2 * chips, rows, LANES), full_type)
-    results = call(
+    part = lambda width: pl.BlockSpec((1, rows, width), lambda i, p: (lax.bitwise_xor(i, p[0] // 2), 0, 0))
+    matrix, vector, router = out((2 * chips, rows, feat), full_type), out((feat,), full_type), out((expert_count, feat), full_type)
+    results = pl.pallas_call(
         assemble_body,
-        (matrix,) * 4 + (small,),
-        "assemble",
-        grid=(2 * chips,),
-        in_specs=[pl.BlockSpec(memory_space=pltpu.SMEM)] + [part(early_width)] * 2 + [part(late_width)] * 2,
-        out_specs=[block(feat)] * 4 + [block(LANES)],
-    )(core, early, early_other, late, late_other)
-    return [a.reshape(feat, a.shape[2]) for a in results]
+        out_shape=(matrix,) * 4 + (router,) + (vector,) * 7,
+        grid_spec=pltpu.PrefetchScalarGridSpec(
+            num_scalar_prefetch=1,
+            grid=(chips,),
+            in_specs=[part(early_width)] * 2 + [part(late_width)] * 2,
+            out_specs=[pl.BlockSpec((2, rows, feat), lambda i, p: (i, 0, 0))] * 4
+            + [pl.BlockSpec((expert_count, feat), lambda i, p: (0, 0))]
+            + [pl.BlockSpec((feat,), lambda i, p: (0,))] * 7,
+            scratch_shapes=[pltpu.VMEM((feat, LANES), full_type)],
+        ),
+        name="assemble",
+        compiler_params=pltpu.CompilerParams(vmem_limit_bytes=vmem_bytes),
+        cost_estimate=pl.CostEstimate(flops=1024, bytes_accessed=1024, transcendentals=0),
+    )(place, early, early_other, late, late_other)
+    return [a.reshape(feat, feat) for a in results[:4]], results[4], results[5:]
 
 
 def widen_body(steps, sum_ref, up_ref, down_ref, up_bias_ref, down_bias_ref):
@@ -967,7 +1001,7 @@
         expert_count,
         capacity,
     )
-    rows = exchange(behind(sent, cot), expert_count)
+    rows = exchange(behind(sent, mark(cot)), expert_count)
     grad_act, start = act_grad(cot, down, expert_down_bias)
     slot = slot_columns(choice_rows, place, capacity, (start,))
     act, grad_pre, gate, score, weight_part = expert(
@@ -1002,7 +1036,7 @@
         bias_parts.append(bias_part)
         group_parts.append(group_part)
         before = (dv, out_blocks)
-    first_blocks = send_blocks(group_parts[0], out_blocks)
+    first_blocks = send_blocks(group_parts[0], mark(out_blocks))
     token_grad, last_part = input_grad(
         grads,
         query_weight,
@@ -1017,20 +1051,22 @@
         group_parts[1],
         (),
     )
-    late = behind(last_part, first_blocks).reshape(expert_count, -1, last_part.shape[1])
+    late = behind(last_part, mark(first_blocks)).reshape(expert_count, -1, last_part.shape[1])
     late = scatter_chips(scatter_step(late, 0, 2))
-    early = jnp.concatenate([sum_blocks(out_blocks), sum_blocks(first_blocks)], axis=1)
+    first_sum = sum_blocks(first_blocks)
+    width = feat // HEAD_GROUPS
+    early = jnp.concatenate([sum_blocks(out_blocks), first_sum[:, : 2 * width]], axis=1)
     returned = exchange(behind(result, late), expert_count)
+    late = jnp.concatenate([late, first_sum[:, 2 * width :]], axis=1)
     share, steps = feat // replicas, up.shape[1] // feat
     up_grad, down_grad, up_bias_grad, down_bias_grad = widen(expert_sum, steps, share)
     block_output = block_result(returned, slot, probs, middle, expert_count, (token_grad,))
     early, late = gather_chips(sum_replicas([early, late], (up_grad,)), (block_output,))
     early, late = together([early, late])
-    core = (lax.axis_index("expert") & 1).reshape(1)
-    out_grad, query_grad, key_grad, value_grad, small = assemble(
-        core, early, swap(early, "expert", 0), late, swap(late, "expert", 0)
+    place_here = lax.axis_index("expert").reshape(1)
+    (out_grad, query_grad, key_grad, value_grad), router_grad, vectors = assemble(
+        place_here, early, swap(early, "expert", 0), late, swap(late, "expert", 0), expert_count
     )
-    vectors = small[:, 32:40].T
     return (
         block_output,
         token_grad,
@@ -1045,7 +1081,7 @@
         vectors[6],
         vectors[4],
         vectors[5],
-        small[:, :expert_count],
+        router_grad.T,
         up_grad[None],
         up_bias_grad,
         down_grad[None],

time: 432 us -> 423 us (0.979)
    pallas_call x14 -> x13, Pallas kernels: 233 us -> 223 us  [build(): pl.pallas_call(inner, out_shape=out_shape, name=name, grid=grid, in_specs...]
    select_n x4 -> x0, other arithmetic: 9.28 us -> none  [gather_chips(): pair[k] = jnp.where(place >> bit & 1 == 0, lower, upper)]
    concatenate x1 -> x6, other arithmetic: 0.76 us -> 9.71 us  [the longest x4 8.18 us: gather_chips(): jnp.concatenate([v, o], axis=len(bits) - bit)]
    pallas_call x0 -> x1, Pallas kernels: none -> 6.64 us  [assemble(): pl.pallas_call(assemble_body, out_shape=(matrix,) * 4 + (router,) + (vect...]
  transfers between devices with their start and end apart: 21 -> 21, of which waited for: 13 -> 12; matrix products, arithmetic and copies ran while one was open for 5% -> 6% of each run, Pallas kernels for 38% -> 39%
where the time goes in v1:
time: 423 us; the launch traced here: 415 us
  Pallas kernels  230 us (54%)
  waiting for transfers between devices  92.6 us (22%)
  starting transfers between devices  41.2 us (10%)
  other arithmetic  20.1 us (5%)
  local copies, waits for them, and re-layouts  17.4 us (4%)
  between operations  14.4 us (3%)
    pallas_call x13, Pallas kernels, build(): pl.pallas_call(inner, out_shape=out_shape, name=name, grid=grid, in_specs...  223 us
    all_to_all x4, waiting for transfers between devices, exchange(): lax.all_to_all(split, 'expert', split_axis=0, concat_axis=0, tiled=True)  49.7 us
    ppermute x10, waiting for transfers between devices, swap(): return lax.ppermute(values, axis, [(i, i ^ 1 << bit) for i in range(count)])  29.8 us
    all_to_all x4, starting transfers between devices, exchange(): lax.all_to_all(split, 'expert', split_axis=0, concat_axis=0, tiled=True)  16.4 us
    ppermute x4, waiting for transfers between devices, scatter_step(): lax.ppermute(part, 'expert', [(i, i ^ step << low) for i in range(lax.axi...  13 us
    ppermute x10, starting transfers between devices, swap(): return lax.ppermute(values, axis, [(i, i ^ 1 << bit) for i in range(count)])  12.6 us
    unnamed x36, local copies, waits for them, and re-layouts  11.5 us
  transfers between devices with their start and end apart: 21, of which 12 were waited for; matrix products, arithmetic and copies ran while one was open for 6% of the time, Pallas kernels for 39%

profile of v1, /device:TPU:0, one launch (start us, length us, event | category | flops | bytes accessed | tf_op | source)
XLA Modules:
  0.0 415.3 jit_solution(7834103115518294408)
XLA Ops:
  7.2 7.3 %route.1 = (s32[32,968]{1,0:T(8,128)}, bf16[2048,768]{1,0:T(8,128)(2,1)}) custom-call(s32[2,968]{1,0:T(2,128)} %bitcast.65, s32[1,968]{1,0:T(1,128)} %refs_1_.2, bf16[968,768]{1,0:T(8,128)(2,1)} %refs_4_.3), custom_call_target="tpu_custom_call" | custom-call | flops 1024 | bytes 1024 | tf_op jit(solution)/shard_map/route/pallas_call | solution.py:85
  14.5 5.3 %all-to-all-start = ((bf16[8,256,768]{2,1,0:T(8,128)(2,1)}), bf16[8,256,768]{2,1,0:T(8,128)(2,1)S(1)}, u32[]{:S(2)}, u32[]{:S(2)}) async-start(bf16[8,256,768]{2,1,0:T(8,128)(2,1)} %bitcast.62), calls=%async_computation | async-start | bytes 6291456 | tf_op jit(solution)/shard_map/all_to_all | solution.py:814
  20.0 0.7 pad.4.refs_12_.refs_7_
  20.7 31.2 %front.1 = (bf16[968,768]{1,0:T(8,128)(2,1)}, bf16[968,768]{1,0:T(8,128)(2,1)}, bf16[968,768]{1,0:T(8,128)(2,1)}, bf16[968,768]{1,0:T(8,128)(2,1)}, f32[12,576]{...) custom-call(bf16[968,768]{1,0:T(8,128)(2,1)} %refs_9_.5, ...), custom_call_target="tpu_custom_call" | custom-call | flops 1024 | bytes 1024 | tf_op jit(solution)/shard_map/front/pallas_call | solution.py:85
  51.9 5.8 %all-to-all-done = bf16[8,256,768]{2,1,0:T(8,128)(2,1)S(1)} async-done(((bf16[8,256,768]{2,1,0:T(8,128)(2,1)}), bf16[8,256,768]{2,1,0:T(8,128)(2,1)S(1)}, u32[]{:S(2)}, u32[]{:S(2)}) %all-to-all-start) | async-done | bytes 3145760 | tf_op jit(solution)/shard_map/all_to_all | solution.py:814
  57.7 0.6 slice.20.refs_1_
  58.3 1.1 copy-done.1
  59.4 3.7 all-to-all-start.1
  63.1 19.0 %act_grad.1 = (bf16[2048,3072]{1,0:T(8,128)(2,1)}, f32[2048,128]{1,0:T(8,128)}) custom-call(bf16[2048,768]{1,0:T(8,128)(2,1)} %bitcast.44, bf16[3072,768]{1,0:T(8,128)(2,1)} %bitcast.46, f32[1,768]{1,0:T(1,128)} %refs_2_.9), custom_call_target="tpu_custom_call" | custom-call | flops 1024 | bytes 1024 | tf_op jit(solution)/shard_map/act_grad/pallas_call | solution.py:85
  82.2 2.0 slot_columns.1.refs_4_.refs_1_
  84.2 18.8 %all-to-all-done.1 = bf16[8,272,768]{2,1,0:T(8,128)(2,1)S(1)} async-done(((bf16[8,272,768]{2,1,0:T(8,128)(2,1)}), bf16[8,272,768]{2,1,0:T(8,128)(2,1)S(1)}, u32[]{:S(2)}, u32[]{:S(2)}) %all-to-all-start.1) | async-done | bytes 3342368 | tf_op jit(solution)/shard_map/all_to_all | solution.py:814
  103.0 1.7 copy-done.3
  104.7 53.4 %expert.1 = (bf16[2048,3072]{1,0:T(8,128)(2,1)}, bf16[2048,3072]{1,0:T(8,128)(2,1)}, f32[2048,128]{1,0:T(8,128)}, f32[2048,128]{1,0:T(8,128)}, bf16[4,1552,768]{2,1,0:T(8,128)(2,1)}) custom-call(bf16[2176,768]{1,0:T(8,128)(2,1)} %bitcast.50, bf16[768,3072]{1,0:T(8,128)(2,1)} %bitcast.60, f32[1,3072]{1,0:T(1,128)} %refs_2_.8, ...), custom_call_target="tpu_custom_call" | custom-call | flops 1024 | bytes 1024 | tf_op jit(solution)/shard_map/expert/pallas_call | solution.py:85
  158.2 15.5 %grad_in.1.refs_3_ = bf16[2176,768]{1,0:T(8,128)(2,1)} custom-call(bf16[2048,3072]{1,0:T(8,128)(2,1)} %get-tuple-element.86.refs_0_, bf16[768,3072]{1,0:T(8,128)(2,1)} %bitcast.61, f32[2048,128]{1,0:T(8,128)} %get-tuple-element.87.refs_2_, f32[2048,128]{1,0:T(8,128)} %get-tuple-element.88.refs_3_, s32[968,2]{1,0:T(8,128)} %slot_columns.1.refs_4_.refs_1_), custom_call_target="tpu_custom_call" | custom-call | flops 399999991808 | bytes 1024 | tf_op jit(solution)/shard_map/grad_in/pallas_call | solution.py:85
  173.7 3.7 all-to-all-start.2
  177.4 14.8 %result.1.refs_10_.refs_0_ = bf16[2048,768]{1,0:T(8,128)(2,1)} custom-call(bf16[2048,3072]{1,0:T(8,128)(2,1)} %get-tuple-element.85.refs_0_, bf16[3072,768]{1,0:T(8,128)(2,1)} %bitcast.47, f32[1,768]{1,0:T(1,128)} %refs_2_.9, bf16[2176,768]{1,0:T(8,128)(2,1)} %grad_in.1.refs_3_), custom_call_target="tpu_custom_call" | custom-call | flops 1024 | bytes 1024 | tf_op jit(solution)/shard_map/result/pallas_call | solution.py:85
  192.1 25.2 %all-to-all-done.2 = bf16[8,272,768]{2,1,0:T(8,128)(2,1)S(1)} async-done(((bf16[8,272,768]{2,1,0:T(8,128)(2,1)}), bf16[8,272,768]{2,1,0:T(8,128)(2,1)S(1)}, u32[]{:S(2)}, u32[]{:S(2)}) %all-to-all-start.2) | async-done | bytes 3342368 | tf_op jit(solution)/shard_map/all_to_all | solution.py:814
  217.3 1.7 copy-done
  219.0 17.7 %combine.1 = (f32[968,768]{1,0:T(8,128)}, bf16[968,768]{1,0:T(8,128)(2,1)}, bf16[768,768]{1,0:T(8,128)(2,1)}, f32[768,128]{1,0:T(8,128)}, f32[3,768]{1,0:T(4,128)}) custom-call(bf16[2176,768]{1,0:T(8,128)(2,1)} %bitcast.41, s32[968,2]{1,0:T(8,128)} %slot_columns.1.refs_4_.refs_1_, f32[968,128]{1,0:T(8,128)} %get-tuple-element.92.refs_2_, ...), custom_call_target="tpu_custom_call" | custom-call | flops 1024 | bytes 1024 | tf_op jit(solution)/shard_map/combine/pallas_call | solution.py:85
  236.6 4.0 all-to-all-start.3
  240.6 17.4 %attention_grad_0.1 = (bf16[968,384]{1,0:T(8,128)(2,1)}, bf16[968,384]{1,0:T(8,128)(2,1)}, bf16[968,384]{1,0:T(8,128)(2,1)}, bf16[768,1152]{1,0:T(8,128)(2,1)}, f32[2,384]{1,0:T(2,128)}) custom-call(bf16[968,768]{1,0:T(8,128)(2,1)} %get-tuple-element.89.refs_0_, bf16[968,768]{1,0:T(8,128)(2,1)} %get-tuple-element.90.refs_1_, ...), custom_call_target="tpu_custom_call" | custom-call | flops 1024 | bytes 1024 | tf_op jit(solution)/shard_map/attention_grad_0/pallas_call | solution.py:85
  258.0 0.6 slice.21.refs_1_
  259.0 4.2 %all-to-all-start.4 = ((bf16[8,96,1152]{2,1,0:T(8,128)(2,1)}), bf16[8,96,1152]{2,1,0:T(8,128)(2,1)S(1)}, u32[]{:S(2)}, u32[]{:S(2)}) async-start(bf16[8,96,1152]{2,1,0:T(8,128)(2,1)} %bitcast.58), calls=%async_computation.4 | async-start | bytes 3538944 | tf_op jit(solution)/shard_map/all_to_all | solution.py:840
  263.2 17.5 %attention_grad_1.1 = (bf16[968,384]{1,0:T(8,128)(2,1)}, bf16[968,384]{1,0:T(8,128)(2,1)}, bf16[968,384]{1,0:T(8,128)(2,1)}, bf16[768,1280]{1,0:T(8,128)(2,1)}, f32[2,384]{1,0:T(2,128)}) custom-call(bf16[968,768]{1,0:T(8,128)(2,1)} %get-tuple-element.89.refs_0_, bf16[968,768]{1,0:T(8,128)(2,1)} %get-tuple-element.90.refs_1_, ...), custom_call_target="tpu_custom_call" | custom-call | flops 1024 | bytes 1024 | tf_op jit(solution)/shard_map/attention_grad_1/pallas_call | solution.py:85
  280.7 11.7 %input_grad.1 = (bf16[968,768]{1,0:T(8,128)(2,1)}, bf16[768,1280]{1,0:T(8,128)(2,1)}) custom-call(bf16[968,384]{1,0:T(8,128)(2,1)} %get-tuple-element.99.refs_0_, bf16[968,384]{1,0:T(8,128)(2,1)} %get-tuple-element.100.refs_1_, bf16[968,384]{1,0:T(8,128)(2,1)} %get-tuple-element.101.refs_7_.refs_2_, ...), custom_call_target="tpu_custom_call", output_to_operand_aliasing={{1}: (16, {})} | custom-call | flops 1024 | bytes 1024 | tf_op jit(solution)/shard_map/input_grad/pallas_call | solution.py:85
  292.3 0.6 slice.22.refs_1_
  293.5 2.4 dynamic-slice_bitcast_fusion
  296.4 2.5 collective-permute-done
  298.9 1.4 fusion
  300.4 0.9 copy-done.11
  301.3 0.8 constant_dynamic-slice_fusion.2
  302.1 1.9 collective-permute-start.1
  304.0 1.5 collective-permute-start.2
  306.1 0.7 pad_maximum_fusion.5.refs_0_
  306.8 4.4 %collective-permute-done.1 = bf16[1,96,1280]{2,1,0:T(8,128)(2,1)} collective-permute-done((bf16[1,96,1280]{2,1,0:T(8,128)(2,1)}, bf16[1,96,1280]{2,1,0:T(8,128)(2,1)}, u32[]{:S(2)}, u32[]{:S(2)}) %collective-permute-start.1) | collective-permute-done | bytes 245792 | tf_op jit(solution)/shard_map/ppermute | solution.py:855
  311.2 6.1 %collective-permute-done.2 = bf16[1,96,1280]{2,1,0:T(8,128)(2,1)} collective-permute-done((bf16[1,96,1280]{2,1,0:T(8,128)(2,1)}, bf16[1,96,1280]{2,1,0:T(8,128)(2,1)}, u32[]{:S(2)}, u32[]{:S(2)}) %collective-permute-start.2) | collective-permute-done | bytes 245792 | tf_op jit(solution)/shard_map/ppermute | solution.py:855
  317.3 1.4 fusion.3.refs_1_
  318.8 0.8 pad_maximum_fusion.4.refs_1_
  319.6 1.6 collective-permute-start.4
  321.2 2.6 collective-permute-start.5
  323.8 3.8 all-to-all-start.5
  327.6 6.6 %collective-permute-done.4 = bf16[96,1536]{1,0:T(8,128)(2,1)} collective-permute-done((bf16[96,1536]{1,0:T(8,128)(2,1)}, bf16[96,1536]{1,0:T(8,128)(2,1)}, u32[]{:S(2)}, u32[]{:S(2)}) %collective-permute-start.4) | collective-permute-done | bytes 294944 | tf_op jit(solution)/shard_map/ppermute | solution.py:820
  334.2 1.8 add_convert_fusion.3.refs_0_
  336.1 1.2 collective-permute-done.5
  337.3 1.8 add_convert_fusion.1.refs_1_
  339.5 3.5 collective-permute-start.6
  342.9 9.0 %collective-permute-done.7 = bf16[96,1664]{1,0:T(8,128)(2,1)S(1)} collective-permute-done((bf16[96,1664]{1,0:T(8,128)(2,1)}, bf16[96,1664]{1,0:T(8,128)(2,1)S(1)}, u32[]{:S(2)}, u32[]{:S(2)}) %collective-permute-start.7) | collective-permute-done | bytes 319520 | tf_op jit(solution)/shard_map/ppermute | solution.py:820
  352.0 1.8 fusion.1.refs_1_
  353.8 4.0 widen.1
  357.8 0.9 copy-done.13
  358.7 1.7 fusion.2.refs_0_
  360.5 1.7 collective-permute-start.8
  362.5 8.4 %collective-permute-done.8 = bf16[1,1,96,1536]{3,2,1,0:T(8,128)(2,1)S(1)} collective-permute-done((bf16[1,1,96,1536]{3,2,1,0:T(8,128)(2,1)}, bf16[1,1,96,1536]{3,2,1,0:T(8,128)(2,1)S(1)}, u32[]{:S(2)}, u32[]{:S(2)}) %collective-permute-start.8) | collective-permute-done | bytes 294944 | tf_op jit(solution)/shard_map/ppermute | solution.py:820
  370.9 1.8 pad_maximum_fusion.3.refs_0_
  372.7 1.9 pad_maximum_fusion.2.refs_1_
  374.6 1.5 collective-permute-start.10
  376.6 1.6 copy-done.4
  378.3 11.4 %block_result.1.refs_1_ = bf16[968,768]{1,0:T(8,128)(2,1)} custom-call(bf16[2048,768]{1,0:T(8,128)(2,1)} %bitcast.53, s32[968,2]{1,0:T(8,128)} %slot_columns.1.refs_4_.refs_1_, f32[968,128]{1,0:T(8,128)} %get-tuple-element.92.refs_2_, f32[968,768]{1,0:T(8,128)} %get-tuple-element.93.refs_3_, bf16[968,768]{1,0:T(8,128)(2,1)} %get-tuple-element.63.refs_4_), custom_call_target="tpu_custom_call" | custom-call | flops 1024 | bytes 1024 | tf_op jit(solution)/shard_map/block_result/pallas_call | solution.py:85
  389.8 1.0 copy-done.10
  390.7 2.2 pad_maximum_fusion.1
  392.9 2.3 pad_maximum_fusion
  395.7 4.4 %collective-permute-done.12.early_other_ref = bf16[4,96,1536]{2,1,0:T(8,128)(2,1)S(1)} collective-permute-done((bf16[4,96,1536]{2,1,0:T(8,128)(2,1)}, bf16[4,96,1536]{2,1,0:T(8,128)(2,1)S(1)}, u32[]{:S(2)}, u32[]{:S(2)}) %collective-permute-start.12) | collective-permute-done | bytes 1179680 | tf_op jit(solution)/shard_map/ppermute | solution.py:820
  400.1 1.1 copy-done.16
  401.6 6.6 %assemble.1 = (f32[8,96,768]{2,1,0:T(8,128)}, f32[8,96,768]{2,1,0:T(8,128)}, f32[8,96,768]{2,1,0:T(8,128)}, f32[8,96,768]{2,1,0:T(8,128)}, f32[8,768]{1,0:T(8,12...) custom-call(s32[1]{0:T(128)} %bitcast.19.place_ref, ...), custom_call_target="tpu_custom_call" | custom-call | flops 1024 | bytes 1024 | tf_op jit(solution)/shard_map/assemble/pallas_call | solution.py:919
  (65 shorter events, 4.6 us)
Async XLA Ops:
  14.5 5.3 %copy-start.17 = (bf16[768,8]{0,1:T(8,128)(2,1)S(1)}, bf16[768,8]{0,1:T(8,128)(2,1)}, u32[]{:S(2)}) copy-start(bf16[768,8]{0,1:T(8,128)(2,1)} %param.32) | copy-start | bytes 36868
  14.5 43.2 %all-to-all-start = ((bf16[8,256,768]{2,1,0:T(8,128)(2,1)}), bf16[8,256,768]{2,1,0:T(8,128)(2,1)S(1)}, u32[]{:S(2)}, u32[]{:S(2)}) async-start(bf16[8,256,768]{2,1,0:T(8,128)(2,1)} %bitcast.62), calls=%async_computation | async-start | bytes 6291456 | tf_op jit(solution)/shard_map/all_to_all | solution.py:814
  57.7 1.8 copy-start.1
  59.4 43.6 %all-to-all-start.1 = ((bf16[8,272,768]{2,1,0:T(8,128)(2,1)}), bf16[8,272,768]{2,1,0:T(8,128)(2,1)S(1)}, u32[]{:S(2)}, u32[]{:S(2)}) async-start(bf16[8,272,768]{2,1,0:T(8,128)(2,1)} %bitcast.52), calls=%async_computation.1 | async-start | bytes 6684672 | tf_op jit(solution)/shard_map/all_to_all | solution.py:814
  63.1 290.7 %reduce-scatter.2.cloned.1.call-start = ((), (), s32[]{:S(2)}) async-start(), calls=%async_computation.7 | async-start | bytes 11919360 | tf_op jit(solution)/shard_map/reduce_scatter | solution.py:1010
  103.0 1.7 copy-start.3
  173.7 43.6 %all-to-all-start.2 = ((bf16[8,272,768]{2,1,0:T(8,128)(2,1)}), bf16[8,272,768]{2,1,0:T(8,128)(2,1)S(1)}, u32[]{:S(2)}, u32[]{:S(2)}) async-start(bf16[8,272,768]{2,1,0:T(8,128)(2,1)} %bitcast.51), calls=%async_computation.2 | async-start | bytes 6684672 | tf_op jit(solution)/shard_map/all_to_all | solution.py:814
  217.3 1.7 copy-start
  236.6 21.4 %all-to-all-start.3 = ((bf16[8,96,768]{2,1,0:T(8,128)(2,1)}), bf16[8,96,768]{2,1,0:T(8,128)(2,1)S(1)}, u32[]{:S(2)}, u32[]{:S(2)}) async-start(bf16[8,96,768]{2,1,0:T(8,128)(2,1)} %bitcast.59), calls=%async_computation.3 | async-start | bytes 2359296 | tf_op jit(solution)/shard_map/all_to_all | solution.py:840
  258.0 1.0 copy-start.5
  259.0 33.3 %all-to-all-start.4 = ((bf16[8,96,1152]{2,1,0:T(8,128)(2,1)}), bf16[8,96,1152]{2,1,0:T(8,128)(2,1)S(1)}, u32[]{:S(2)}, u32[]{:S(2)}) async-start(bf16[8,96,1152]{2,1,0:T(8,128)(2,1)} %bitcast.58), calls=%async_computation.4 | async-start | bytes 3538944 | tf_op jit(solution)/shard_map/all_to_all | solution.py:840
  292.3 1.2 copy-start.7
  293.5 5.4 %copy-start.2 = (bf16[768,1280]{1,0:T(8,128)(2,1)S(1)}, bf16[768,1280]{1,0:T(8,128)(2,1)}, u32[]{:S(2)}) copy-start(bf16[768,1280]{1,0:T(8,128)(2,1)} %together.15) | copy-start | bytes 5898244
  295.9 3.0 collective-permute-start
  296.4 9.2 %copy-start.6 = (bf16[8,96,768]{2,1,0:T(8,128)(2,1)S(1)}, bf16[8,96,768]{2,1,0:T(8,128)(2,1)}, u32[]{:S(2)}) copy-start(bf16[8,96,768]{2,1,0:T(8,128)(2,1)} %copy-done.5) | copy-start | bytes 3538948
  300.3 0.9 copy-start.11
  301.3 4.5 %copy-start.8 = (bf16[8,96,1152]{2,1,0:T(8,128)(2,1)S(1)}, bf16[8,96,1152]{2,1,0:T(8,128)(2,1)}, u32[]{:S(2)}) copy-start(bf16[8,96,1152]{2,1,0:T(8,128)(2,1)} %copy-done.7) | copy-start | bytes 5308420
  302.1 9.1 %collective-permute-start.1 = (bf16[1,96,1280]{2,1,0:T(8,128)(2,1)}, bf16[1,96,1280]{2,1,0:T(8,128)(2,1)}, u32[]{:S(2)}, u32[]{:S(2)}) collective-permute-start(bf16[1,96,1280]{2,1,0:T(8,128)(2,1)} %get-tuple-element.142), channel_id=1, source_target_pairs={{0,2},{1,3},{2,0},{3,1},{4,6},{5,7},{6,4},{7,5},{8,10},{9,11},{10,... | collective-permute-start | bytes 737288 | tf_op jit(solution)/shard_map/ppermute | solution.py:855
  304.0 13.3 %collective-permute-start.2 = (bf16[1,96,1280]{2,1,0:T(8,128)(2,1)}, bf16[1,96,1280]{2,1,0:T(8,128)(2,1)}, u32[]{:S(2)}, u32[]{:S(2)}) collective-permute-start(bf16[1,96,1280]{2,1,0:T(8,128)(2,1)} %get-tuple-element.144), channel_id=1, source_target_pairs={{0,4},{1,5},{2,6},{3,7},{4,0},{5,1},{6,2},{7,3},{8,12},{9,13},{10,... | collective-permute-start | bytes 737288 | tf_op jit(solution)/shard_map/ppermute | solution.py:855
  305.5 11.8 %collective-permute-start.3 = (bf16[1,96,1280]{2,1,0:T(8,128)(2,1)S(1)}, bf16[1,96,1280]{2,1,0:T(8,128)(2,1)}, u32[]{:S(2)}, u32[]{:S(2)}) collective-permute-start(bf16[1,96,1280]{2,1,0:T(8,128)(2,1)S(1)} %get-tuple-element.143), channel_id=1, source_target_pairs={{0,6},{1,7},{2,4},{3,5},{4,2},{5,3},{6,0},{7,1},{8,14},{9,15},{10,... | collective-permute-start | bytes 737288 | tf_op jit(solution)/shard_map/ppermute | solution.py:855
  318.8 2.4 copy-start.14
  319.6 1.6 copy-start.12
  319.6 14.7 %collective-permute-start.4 = (bf16[96,1536]{1,0:T(8,128)(2,1)}, bf16[96,1536]{1,0:T(8,128)(2,1)}, u32[]{:S(2)}, u32[]{:S(2)}) collective-permute-start(bf16[96,1536]{1,0:T(8,128)(2,1)} %get-tuple-element.115), channel_id=1, source_target_pairs={{0,8},{8,0},{16,24},{24,16},{1,9},{9,1},{17,25},{25,17},{2,10},{10... | collective-permute-start | bytes 884744 | tf_op jit(solution)/shard_map/ppermute | solution.py:820
  321.2 16.1 %collective-permute-start.5 = (bf16[96,1664]{1,0:T(8,128)(2,1)S(1)}, bf16[96,1664]{1,0:T(8,128)(2,1)}, u32[]{:S(2)}, u32[]{:S(2)}) collective-permute-start(bf16[96,1664]{1,0:T(8,128)(2,1)S(1)} %copy-done.12), channel_id=1, source_target_pairs={{0,16},{8,24},{16,0},{24,8},{1,17},{9,25},{17,1},{25,9},{2,18},{10... | collective-permute-start | bytes 958472 | tf_op jit(solution)/shard_map/ppermute | solution.py:820
  323.8 52.8 %all-to-all-start.5 = ((bf16[8,256,768]{2,1,0:T(8,128)(2,1)}), bf16[8,256,768]{2,1,0:T(8,128)(2,1)S(1)}, u32[]{:S(2)}, u32[]{:S(2)}) async-start(bf16[8,256,768]{2,1,0:T(8,128)(2,1)} %bitcast.40), calls=%async_computation.5 | async-start | bytes 6291456 | tf_op jit(solution)/shard_map/all_to_all | solution.py:814
  339.1 12.9 %collective-permute-start.7 = (bf16[96,1664]{1,0:T(8,128)(2,1)}, bf16[96,1664]{1,0:T(8,128)(2,1)S(1)}, u32[]{:S(2)}, u32[]{:S(2)}) collective-permute-start(bf16[96,1664]{1,0:T(8,128)(2,1)} %get-tuple-element.120), channel_id=1, source_target_pairs={{0,8},{8,0},{16,24},{24,16},{1,9},{9,1},{17,25},{25,17},{2,10},{10... | collective-permute-start | bytes 958472 | tf_op jit(solution)/shard_map/ppermute | solution.py:820
  339.5 18.3 %collective-permute-start.6 = (bf16[96,1536]{1,0:T(8,128)(2,1)}, bf16[96,1536]{1,0:T(8,128)(2,1)}, u32[]{:S(2)}, u32[]{:S(2)}) collective-permute-start(bf16[96,1536]{1,0:T(8,128)(2,1)} %get-tuple-element.117), channel_id=1, source_target_pairs={{0,16},{8,24},{16,0},{24,8},{1,17},{9,25},{17,1},{25,9},{2,18},{10... | collective-permute-start | bytes 884744 | tf_op jit(solution)/shard_map/ppermute | solution.py:820
  357.8 1.0 copy-start.13
  360.5 10.4 %collective-permute-start.8 = (bf16[1,1,96,1536]{3,2,1,0:T(8,128)(2,1)}, bf16[1,1,96,1536]{3,2,1,0:T(8,128)(2,1)S(1)}, u32[]{:S(2)}, u32[]{:S(2)}) collective-permute-start(bf16[1,1,96,1536]{3,2,1,0:T(8,128)(2,1)} %get-tuple-element.121), channel_id=1, source_target_pairs={{0,2},{1,3},{2,0},{3,1},{4,6},{5,7},{6,4},{7,5},{8,10},{9,11},{10,... | collective-permute-start | bytes 884744 | tf_op jit(solution)/shard_map/ppermute | solution.py:820
  362.1 10.6 %collective-permute-start.9 = (bf16[1,1,96,1664]{3,2,1,0:T(8,128)(2,1)}, bf16[1,1,96,1664]{3,2,1,0:T(8,128)(2,1)S(1)}, u32[]{:S(2)}, u32[]{:S(2)}) collective-permute-start(bf16[1,1,96,1664]{3,2,1,0:T(8,128)(2,1)} %get-tuple-element.122), channel_id=1, source_target_pairs={{0,4},{1,5},{2,6},{3,7},{4,0},{5,1},{6,2},{7,3},{8,12},{9,13},{10,... | collective-permute-start | bytes 958472 | tf_op jit(solution)/shard_map/ppermute | solution.py:820
  374.6 15.2 %collective-permute-start.10 = (bf16[1,2,96,1536]{3,2,1,0:T(8,128)(2,1)}, bf16[1,2,96,1536]{3,2,1,0:T(8,128)(2,1)}, u32[]{:S(2)}, u32[]{:S(2)}) collective-permute-start(bf16[1,2,96,1536]{3,2,1,0:T(8,128)(2,1)} %get-tuple-element.123), channel_id=1, source_target_pairs={{0,4},{1,5},{2,6},{3,7},{4,0},{5,1},{6,2},{7,3},{8,12},{9,13},{10,... | collective-permute-start | bytes 1769480 | tf_op jit(solution)/shard_map/ppermute | solution.py:820
  376.1 16.8 %collective-permute-start.11 = (bf16[2,1,96,1664]{3,2,1,0:T(8,128)(2,1)}, bf16[2,1,96,1664]{3,2,1,0:T(8,128)(2,1)}, u32[]{:S(2)}, u32[]{:S(2)}) collective-permute-start(bf16[2,1,96,1664]{3,2,1,0:T(8,128)(2,1)} %get-tuple-element.124), channel_id=1, source_target_pairs={{0,2},{1,3},{2,0},{3,1},{4,6},{5,7},{6,4},{7,5},{8,10},{9,11},{10,... | collective-permute-start | bytes 1916936 | tf_op jit(solution)/shard_map/ppermute | solution.py:820
  376.6 1.6 copy-start.4
  389.7 1.1 copy-start.10
  389.7 3.3 copy-start.9
  395.2 4.9 %collective-permute-start.13 = (bf16[4,96,1664]{2,1,0:T(8,128)(2,1)}, bf16[4,96,1664]{2,1,0:T(8,128)(2,1)S(1)}, u32[]{:S(2)}, u32[]{:S(2)}) collective-permute-start(bf16[4,96,1664]{2,1,0:T(8,128)(2,1)} %get-tuple-element.126.late_ref), channel_id=1, source_target_pairs={{0,1},{1,0},{2,3},{3,2},{4,5},{5,4},{6,7},{7,6},{8,9},{9,8},{10,11... | collective-permute-start | bytes 3833864 | tf_op jit(solution)/shard_map/ppermute | solution.py:820
  395.2 4.9 %collective-permute-start.12 = (bf16[4,96,1536]{2,1,0:T(8,128)(2,1)}, bf16[4,96,1536]{2,1,0:T(8,128)(2,1)S(1)}, u32[]{:S(2)}, u32[]{:S(2)}) collective-permute-start(bf16[4,96,1536]{2,1,0:T(8,128)(2,1)} %get-tuple-element.125.early_ref), channel_id=1, source_target_pairs={{0,1},{1,0},{2,3},{3,2},{4,5},{5,4},{6,7},{7,6},{8,9},{9,8},{10,11... | collective-permute-start | bytes 3538952 | tf_op jit(solution)/shard_map/ppermute | solution.py:820
  400.1 1.1 copy-start.16
  400.1 1.5 copy-start.15
Sparse Core Ops, SparseCore 0:
  158.3 162.5 reduce-scatter.1

commit v2 on v1

--- a/solution.py
+++ b/solution.py
@@ -877,44 +877,64 @@
         pair = together(pair)
         steps = [bits[n], bits[-1 - n]]
         others = [swap(v, "expert", bit) for v, bit in zip(pair, steps)]
-        if n == len(bits) - 1 and fill:
-            others[0] = behind(others[0], *fill)
-        pair = [jnp.concatenate([v, o], axis=len(bits) - bit) for v, o, bit in zip(pair, others, steps)]
-    return [v.reshape(-1, *shape) for v, shape in zip(pair, shapes)]
-
-
-def assemble_body(place_ref, early_ref, early_other_ref, late_ref, late_other_ref, *refs):
+        if n < len(bits) - 1:
+            pair = [jnp.concatenate([v, o], axis=len(bits) - bit) for v, o, bit in zip(pair, others, steps)]
+    if fill:
+        others = together(others, fill)
+    return [[a.reshape(-1, *shape) for a in both] for *both, shape in zip(pair, others, shapes)]
+
+
+def assemble_body(place_ref, *refs):
+    pieces, refs = refs[:8], refs[8:]
     out_ref, query_ref, key_ref, value_ref, router_ref = refs[:5]
     vector_refs, held_ref = refs[5:-1], refs[-1]
     rows, feat = out_ref.shape[1:]
     width = feat // HEAD_GROUPS
     own = lax.rem(place_ref[0], 2)
-    number = pl.program_id(0)
-    for core, early_part, late_part in ((own, early_ref, late_ref), (1 - own, early_other_ref, late_other_ref)):
-        early, late = early_part[0].astype(full_type), late_part[0].astype(full_type)
+    number, chips = pl.program_id(0), pl.num_programs(0)
+    chip = lax.bitwise_xor(number, place_ref[0] // 2)
+
+    def early_part(core, ref):
+        early = ref[0].astype(full_type)
         out_ref[core] = early[:, :feat]
-        for kind, ref in enumerate((query_ref, key_ref, value_ref)):
-            start = kind * width
-            moved = feat + start if kind < 2 else 3 * width + LANES
-            ref[core, :, :width] = (early if kind < 2 else late)[:, moved : moved + width]
-            ref[core, :, width:] = late[:, start : start + width]
+        query_ref[core, :, :width] = early[:, feat : feat + width]
+        key_ref[core, :, :width] = early[:, feat + width :]
+
+    def late_part(core, ref):
+        late = ref[0].astype(full_type)
+        for kind, target in enumerate((query_ref, key_ref, value_ref)):
+            target[core, :, width:] = late[:, kind * width : kind * width + width]
+        value_ref[core, :, :width] = late[:, 3 * width + LANES :]
         small = late[:, 3 * width : 3 * width + LANES]
-        held_ref[pl.ds(pl.multiple_of((2 * number + core) * rows, 8), rows), :] = small
-
-    @pl.when(number == pl.num_programs(0) - 1)
+        held_ref[pl.ds(pl.multiple_of((2 * chip + core) * rows, 8), rows), :] = small
+
+    for core, side in ((own, 0), (1 - own, 4)):
+        for half in range(2):
+
+            @pl.when((number >= chips // 2) == (half == 1))
+            def _():
+                early_part(core, pieces[side + half])
+
+            @pl.when((lax.rem(number, 2) == 1) == (half == 1))
+            def _():
+                late_part(core, pieces[side + 2 + half])
+
+    @pl.when(number == chips - 1)
     def _():
-        small = held_ref[...]
-        columns = small.T
+        columns = held_ref[...].T
         router_ref[...] = columns[: router_ref.shape[0]]
         for k, ref in enumerate(vector_refs):
             ref[...] = columns[32 + k]
 
 
-def assemble(place, early, early_other, late, late_other, expert_count):
-    chips, rows, early_width = early.shape
-    late_width = late.shape[2]
+def assemble(place, own, other, expert_count):
+    half, rows, early_width = own[0].shape
+    late_width = own[2].shape[2]
+    chips = 2 * half
     feat = 2 * chips * rows
-    part = lambda width: pl.BlockSpec((1, rows, width), lambda i, p: (lax.bitwise_xor(i, p[0] // 2), 0, 0))
+    first = pl.BlockSpec((1, rows, early_width), lambda i, p: (jnp.minimum(i, half - 1), 0, 0))
+    second = pl.BlockSpec((1, rows, early_width), lambda i, p: (jnp.maximum(i - half, 0), 0, 0))
+    paired = pl.BlockSpec((1, rows, late_width), lambda i, p: (i // 2, 0, 0))
     matrix, vector, router = out((2 * chips, rows, feat), full_type), out((feat,), full_type), out((expert_count, feat), full_type)
     results = pl.pallas_call(
         assemble_body,
@@ -922,8 +942,8 @@
         grid_spec=pltpu.PrefetchScalarGridSpec(
             num_scalar_prefetch=1,
             grid=(chips,),
-            in_specs=[part(early_width)] * 2 + [part(late_width)] * 2,
-            out_specs=[pl.BlockSpec((2, rows, feat), lambda i, p: (i, 0, 0))] * 4
+            in_specs=[first, second, paired, paired] * 2,
+            out_specs=[pl.BlockSpec((2, rows, feat), lambda i, p: (lax.bitwise_xor(i, p[0] // 2), 0, 0))] * 4
             + [pl.BlockSpec((expert_count, feat), lambda i, p: (0, 0))]
             + [pl.BlockSpec((feat,), lambda i, p: (0,))] * 7,
             scratch_shapes=[pltpu.VMEM((feat, LANES), full_type)],
@@ -931,7 +951,7 @@
         name="assemble",
         compiler_params=pltpu.CompilerParams(vmem_limit_bytes=vmem_bytes),
         cost_estimate=pl.CostEstimate(flops=1024, bytes_accessed=1024, transcendentals=0),
-    )(place, early, early_other, late, late_other)
+    )(place, *own, *other)
     return [a.reshape(feat, feat) for a in results[:4]], results[4], results[5:]
 
 
@@ -1062,11 +1082,10 @@
     up_grad, down_grad, up_bias_grad, down_bias_grad = widen(expert_sum, steps, share)
     block_output = block_result(returned, slot, probs, middle, expert_count, (token_grad,))
     early, late = gather_chips(sum_replicas([early, late], (up_grad,)), (block_output,))
-    early, late = together([early, late])
     place_here = lax.axis_index("expert").reshape(1)
-    (out_grad, query_grad, key_grad, value_grad), router_grad, vectors = assemble(
-        place_here, early, swap(early, "expert", 0), late, swap(late, "expert", 0), expert_count
-    )
+    own = [*early, *late]
+    other = [swap(a, "expert", 0) for a in own]
+    (out_grad, query_grad, key_grad, value_grad), router_grad, vectors = assemble(place_here, own, other, expert_count)
     return (
         block_output,
         token_grad,

time: 423 us -> 418 us (0.988)
  other arithmetic: 20.1 us -> 15.6 us
    concatenate x4 -> x2, other arithmetic: 8.18 us -> 3.71 us  [gather_chips(): jnp.concatenate([v, o], axis=len(bits) - bit)]
    unnamed x36 -> x38, local copies, waits for them, and re-layouts: 11.5 us -> 10 us
    ppermute x10 -> x12, waiting for transfers between devices: 29.8 us -> 29.9 us  [swap(): return lax.ppermute(values, axis, [(i, i ^ 1 << bit) for i in range(count)])]
    ppermute x10 -> x12, starting transfers between devices: 12.6 us -> 12.6 us  [swap(): return lax.ppermute(values, axis, [(i, i ^ 1 << bit) for i in range(count)])]
  transfers between devices with their start and end apart: 21 -> 23, of which waited for: 12 -> 14; matrix products, arithmetic and copies ran while one was open for 6% -> 5% of each run, Pallas kernels for 39% -> 40%
where the time goes in v2:
time: 418 us; the launch traced here: 410 us
  Pallas kernels  230 us (55%)
  waiting for transfers between devices  92.7 us (22%)
  starting transfers between devices  41.2 us (10%)
  local copies, waits for them, and re-layouts  16 us (4%)
  other arithmetic  15.6 us (4%)
  between operations  14.4 us (3%)
    pallas_call x13, Pallas kernels, build(): pl.pallas_call(inner, out_shape=out_shape, name=name, grid=grid, in_specs...  223 us
    all_to_all x4, waiting for transfers between devices, exchange(): lax.all_to_all(split, 'expert', split_axis=0, concat_axis=0, tiled=True)  49.8 us
    ppermute x12, waiting for transfers between devices, swap(): return lax.ppermute(values, axis, [(i, i ^ 1 << bit) for i in range(count)])  29.9 us
    all_to_all x4, starting transfers between devices, exchange(): lax.all_to_all(split, 'expert', split_axis=0, concat_axis=0, tiled=True)  16.4 us
    ppermute x4, waiting for transfers between devices, scatter_step(): lax.ppermute(part, 'expert', [(i, i ^ step << low) for i in range(lax.axi...  13 us
    ppermute x12, starting transfers between devices, swap(): return lax.ppermute(values, axis, [(i, i ^ 1 << bit) for i in range(count)])  12.6 us
    unnamed x38, local copies, waits for them, and re-layouts  10 us
  transfers between devices with their start and end apart: 23, of which 14 were waited for; matrix products, arithmetic and copies ran while one was open for 5% of the time, Pallas kernels for 40%

profile of v2, /device:TPU:0, one launch (start us, length us, event | category | flops | bytes accessed | tf_op | source)
XLA Modules:
  0.0 409.6 jit_solution(15222970089162765758)
XLA Ops:
  7.2 7.3 %route.1 = (s32[32,968]{1,0:T(8,128)}, bf16[2048,768]{1,0:T(8,128)(2,1)}) custom-call(s32[2,968]{1,0:T(2,128)} %bitcast.67, s32[1,968]{1,0:T(1,128)} %refs_1_.2, bf16[968,768]{1,0:T(8,128)(2,1)} %refs_4_.3), custom_call_target="tpu_custom_call" | custom-call | flops 1024 | bytes 1024 | tf_op jit(solution)/shard_map/route/pallas_call | solution.py:85
  14.5 5.3 %all-to-all-start = ((bf16[8,256,768]{2,1,0:T(8,128)(2,1)}), bf16[8,256,768]{2,1,0:T(8,128)(2,1)S(1)}, u32[]{:S(2)}, u32[]{:S(2)}) async-start(bf16[8,256,768]{2,1,0:T(8,128)(2,1)} %bitcast.64), calls=%async_computation | async-start | bytes 6291456 | tf_op jit(solution)/shard_map/all_to_all | solution.py:814
  20.0 0.7 pad.4.refs_12_.refs_7_
  20.7 31.2 %front.1 = (bf16[968,768]{1,0:T(8,128)(2,1)}, bf16[968,768]{1,0:T(8,128)(2,1)}, bf16[968,768]{1,0:T(8,128)(2,1)}, bf16[968,768]{1,0:T(8,128)(2,1)}, f32[12,576]{...) custom-call(bf16[968,768]{1,0:T(8,128)(2,1)} %refs_9_.5, ...), custom_call_target="tpu_custom_call" | custom-call | flops 1024 | bytes 1024 | tf_op jit(solution)/shard_map/front/pallas_call | solution.py:85
  51.9 5.8 %all-to-all-done = bf16[8,256,768]{2,1,0:T(8,128)(2,1)S(1)} async-done(((bf16[8,256,768]{2,1,0:T(8,128)(2,1)}), bf16[8,256,768]{2,1,0:T(8,128)(2,1)S(1)}, u32[]{:S(2)}, u32[]{:S(2)}) %all-to-all-start) | async-done | bytes 3145760 | tf_op jit(solution)/shard_map/all_to_all | solution.py:814
  57.7 0.6 slice.20.refs_1_
  58.3 1.1 copy-done.1
  59.4 3.7 all-to-all-start.1
  63.1 19.0 %act_grad.1 = (bf16[2048,3072]{1,0:T(8,128)(2,1)}, f32[2048,128]{1,0:T(8,128)}) custom-call(bf16[2048,768]{1,0:T(8,128)(2,1)} %bitcast.46, bf16[3072,768]{1,0:T(8,128)(2,1)} %bitcast.48, f32[1,768]{1,0:T(1,128)} %refs_2_.9), custom_call_target="tpu_custom_call" | custom-call | flops 1024 | bytes 1024 | tf_op jit(solution)/shard_map/act_grad/pallas_call | solution.py:85
  82.2 2.0 slot_columns.1.refs_4_.refs_1_
  84.2 18.8 %all-to-all-done.1 = bf16[8,272,768]{2,1,0:T(8,128)(2,1)S(1)} async-done(((bf16[8,272,768]{2,1,0:T(8,128)(2,1)}), bf16[8,272,768]{2,1,0:T(8,128)(2,1)S(1)}, u32[]{:S(2)}, u32[]{:S(2)}) %all-to-all-start.1) | async-done | bytes 3342368 | tf_op jit(solution)/shard_map/all_to_all | solution.py:814
  103.0 1.7 copy-done.3
  104.7 53.4 %expert.1 = (bf16[2048,3072]{1,0:T(8,128)(2,1)}, bf16[2048,3072]{1,0:T(8,128)(2,1)}, f32[2048,128]{1,0:T(8,128)}, f32[2048,128]{1,0:T(8,128)}, bf16[4,1552,768]{2,1,0:T(8,128)(2,1)}) custom-call(bf16[2176,768]{1,0:T(8,128)(2,1)} %bitcast.52, bf16[768,3072]{1,0:T(8,128)(2,1)} %bitcast.62, f32[1,3072]{1,0:T(1,128)} %refs_2_.8, ...), custom_call_target="tpu_custom_call" | custom-call | flops 1024 | bytes 1024 | tf_op jit(solution)/shard_map/expert/pallas_call | solution.py:85
  158.1 15.5 %grad_in.1.refs_3_ = bf16[2176,768]{1,0:T(8,128)(2,1)} custom-call(bf16[2048,3072]{1,0:T(8,128)(2,1)} %get-tuple-element.86.refs_0_, bf16[768,3072]{1,0:T(8,128)(2,1)} %bitcast.63, f32[2048,128]{1,0:T(8,128)} %get-tuple-element.87.refs_2_, f32[2048,128]{1,0:T(8,128)} %get-tuple-element.88.refs_3_, s32[968,2]{1,0:T(8,128)} %slot_columns.1.refs_4_.refs_1_), custom_call_target="tpu_custom_call" | custom-call | flops 399999991808 | bytes 1024 | tf_op jit(solution)/shard_map/grad_in/pallas_call | solution.py:85
  173.7 3.7 all-to-all-start.2
  177.3 14.7 %result.1.refs_10_.refs_0_ = bf16[2048,768]{1,0:T(8,128)(2,1)} custom-call(bf16[2048,3072]{1,0:T(8,128)(2,1)} %get-tuple-element.85.refs_0_, bf16[3072,768]{1,0:T(8,128)(2,1)} %bitcast.49, f32[1,768]{1,0:T(1,128)} %refs_2_.9, bf16[2176,768]{1,0:T(8,128)(2,1)} %grad_in.1.refs_3_), custom_call_target="tpu_custom_call" | custom-call | flops 1024 | bytes 1024 | tf_op jit(solution)/shard_map/result/pallas_call | solution.py:85
  192.1 25.2 %all-to-all-done.2 = bf16[8,272,768]{2,1,0:T(8,128)(2,1)S(1)} async-done(((bf16[8,272,768]{2,1,0:T(8,128)(2,1)}), bf16[8,272,768]{2,1,0:T(8,128)(2,1)S(1)}, u32[]{:S(2)}, u32[]{:S(2)}) %all-to-all-start.2) | async-done | bytes 3342368 | tf_op jit(solution)/shard_map/all_to_all | solution.py:814
  217.3 1.7 copy-done
  218.9 17.7 %combine.1 = (f32[968,768]{1,0:T(8,128)}, bf16[968,768]{1,0:T(8,128)(2,1)}, bf16[768,768]{1,0:T(8,128)(2,1)}, f32[768,128]{1,0:T(8,128)}, f32[3,768]{1,0:T(4,128)}) custom-call(bf16[2176,768]{1,0:T(8,128)(2,1)} %bitcast.43, s32[968,2]{1,0:T(8,128)} %slot_columns.1.refs_4_.refs_1_, f32[968,128]{1,0:T(8,128)} %get-tuple-element.92.refs_2_, ...), custom_call_target="tpu_custom_call" | custom-call | flops 1024 | bytes 1024 | tf_op jit(solution)/shard_map/combine/pallas_call | solution.py:85
  236.6 4.0 all-to-all-start.3
  240.6 17.4 %attention_grad_0.1 = (bf16[968,384]{1,0:T(8,128)(2,1)}, bf16[968,384]{1,0:T(8,128)(2,1)}, bf16[968,384]{1,0:T(8,128)(2,1)}, bf16[768,1152]{1,0:T(8,128)(2,1)}, f32[2,384]{1,0:T(2,128)}) custom-call(bf16[968,768]{1,0:T(8,128)(2,1)} %get-tuple-element.89.refs_0_, bf16[968,768]{1,0:T(8,128)(2,1)} %get-tuple-element.90.refs_1_, ...), custom_call_target="tpu_custom_call" | custom-call | flops 1024 | bytes 1024 | tf_op jit(solution)/shard_map/attention_grad_0/pallas_call | solution.py:85
  258.0 0.6 slice.21.refs_1_
  259.0 4.2 %all-to-all-start.4 = ((bf16[8,96,1152]{2,1,0:T(8,128)(2,1)}), bf16[8,96,1152]{2,1,0:T(8,128)(2,1)S(1)}, u32[]{:S(2)}, u32[]{:S(2)}) async-start(bf16[8,96,1152]{2,1,0:T(8,128)(2,1)} %bitcast.58), calls=%async_computation.4 | async-start | bytes 3538944 | tf_op jit(solution)/shard_map/all_to_all | solution.py:840
  263.2 17.5 %attention_grad_1.1 = (bf16[968,384]{1,0:T(8,128)(2,1)}, bf16[968,384]{1,0:T(8,128)(2,1)}, bf16[968,384]{1,0:T(8,128)(2,1)}, bf16[768,1280]{1,0:T(8,128)(2,1)}, f32[2,384]{1,0:T(2,128)}) custom-call(bf16[968,768]{1,0:T(8,128)(2,1)} %get-tuple-element.89.refs_0_, bf16[968,768]{1,0:T(8,128)(2,1)} %get-tuple-element.90.refs_1_, ...), custom_call_target="tpu_custom_call" | custom-call | flops 1024 | bytes 1024 | tf_op jit(solution)/shard_map/attention_grad_1/pallas_call | solution.py:85
  280.6 11.7 %input_grad.1 = (bf16[968,768]{1,0:T(8,128)(2,1)}, bf16[768,1280]{1,0:T(8,128)(2,1)}) custom-call(bf16[968,384]{1,0:T(8,128)(2,1)} %get-tuple-element.99.refs_0_, bf16[968,384]{1,0:T(8,128)(2,1)} %get-tuple-element.100.refs_1_, bf16[968,384]{1,0:T(8,128)(2,1)} %get-tuple-element.101.refs_7_.refs_2_, ...), custom_call_target="tpu_custom_call", output_to_operand_aliasing={{1}: (16, {})} | custom-call | flops 1024 | bytes 1024 | tf_op jit(solution)/shard_map/input_grad/pallas_call | solution.py:85
  292.3 0.6 slice.22.refs_1_
  293.0 0.6 copy-done.7
  293.5 2.4 dynamic-slice_bitcast_fusion
  296.4 2.5 collective-permute-done
  298.9 1.4 fusion
  300.3 0.9 copy-done.10
  301.3 0.8 constant_dynamic-slice_fusion.2
  302.1 1.9 collective-permute-start.1
  304.0 1.5 collective-permute-start.2
  306.1 0.7 pad_maximum_fusion.3.refs_0_
  306.8 4.4 %collective-permute-done.1 = bf16[1,96,1280]{2,1,0:T(8,128)(2,1)} collective-permute-done((bf16[1,96,1280]{2,1,0:T(8,128)(2,1)}, bf16[1,96,1280]{2,1,0:T(8,128)(2,1)}, u32[]{:S(2)}, u32[]{:S(2)}) %collective-permute-start.1) | collective-permute-done | bytes 245792 | tf_op jit(solution)/shard_map/ppermute | solution.py:855
  311.2 6.1 %collective-permute-done.2 = bf16[1,96,1280]{2,1,0:T(8,128)(2,1)} collective-permute-done((bf16[1,96,1280]{2,1,0:T(8,128)(2,1)}, bf16[1,96,1280]{2,1,0:T(8,128)(2,1)}, u32[]{:S(2)}, u32[]{:S(2)}) %collective-permute-start.2) | collective-permute-done | bytes 245792 | tf_op jit(solution)/shard_map/ppermute | solution.py:855
  317.3 1.4 fusion.3.refs_1_
  318.7 0.8 pad_maximum_fusion.2.refs_1_
  319.5 1.6 collective-permute-start.4
  321.1 2.6 collective-permute-start.5
  323.8 3.8 all-to-all-start.5
  327.6 6.7 %collective-permute-done.4 = bf16[96,1536]{1,0:T(8,128)(2,1)} collective-permute-done((bf16[96,1536]{1,0:T(8,128)(2,1)}, bf16[96,1536]{1,0:T(8,128)(2,1)}, u32[]{:S(2)}, u32[]{:S(2)}) %collective-permute-start.4) | collective-permute-done | bytes 294944 | tf_op jit(solution)/shard_map/ppermute | solution.py:820
  334.2 1.8 add_convert_fusion.3.refs_0_
  336.1 1.2 collective-permute-done.5
  337.3 1.8 add_convert_fusion.1.refs_1_
  339.4 3.5 collective-permute-start.6
  342.9 9.1 %collective-permute-done.7 = bf16[96,1664]{1,0:T(8,128)(2,1)S(1)} collective-permute-done((bf16[96,1664]{1,0:T(8,128)(2,1)}, bf16[96,1664]{1,0:T(8,128)(2,1)S(1)}, u32[]{:S(2)}, u32[]{:S(2)}) %collective-permute-start.7) | collective-permute-done | bytes 319520 | tf_op jit(solution)/shard_map/ppermute | solution.py:820
  352.0 1.8 fusion.1.refs_1_
  353.8 4.0 widen.1
  357.8 0.9 copy-done.12
  358.7 1.7 fusion.2.refs_0_
  360.5 1.7 collective-permute-start.8
  362.5 8.3 %collective-permute-done.8 = bf16[1,1,96,1536]{3,2,1,0:T(8,128)(2,1)S(1)} collective-permute-done((bf16[1,1,96,1536]{3,2,1,0:T(8,128)(2,1)}, bf16[1,1,96,1536]{3,2,1,0:T(8,128)(2,1)S(1)}, u32[]{:S(2)}, u32[]{:S(2)}) %collective-permute-start.8) | collective-permute-done | bytes 294944 | tf_op jit(solution)/shard_map/ppermute | solution.py:820
  370.8 1.8 pad_maximum_fusion.1.refs_0_
  372.7 1.9 pad_maximum_fusion.refs_1_
  374.9 1.7 collective-permute-start.10
  376.6 1.6 copy-done.4
  378.2 11.4 %block_result.1.refs_2_ = bf16[968,768]{1,0:T(8,128)(2,1)} custom-call(bf16[2048,768]{1,0:T(8,128)(2,1)} %bitcast.55, s32[968,2]{1,0:T(8,128)} %slot_columns.1.refs_4_.refs_1_, f32[968,128]{1,0:T(8,128)} %get-tuple-element.92.refs_2_, f32[968,768]{1,0:T(8,128)} %get-tuple-element.93.refs_3_, bf16[968,768]{1,0:T(8,128)(2,1)} %get-tuple-element.63.refs_4_), custom_call_target="tpu_custom_call" | custom-call | flops 1024 | bytes 1024 | tf_op jit(solution)/shard_map/block_result/pallas_call | solution.py:85
  389.8 1.0 collective-permute-done.11.refs_1_
  390.8 0.5 collective-permute-start.12
  391.3 2.9 collective-permute-done.12.refs_4_
  394.2 0.6 collective-permute-done.13.refs_5_
  395.8 6.7 %assemble.1 = (f32[8,96,768]{2,1,0:T(8,128)}, f32[8,96,768]{2,1,0:T(8,128)}, f32[8,96,768]{2,1,0:T(8,128)}, f32[8,96,768]{2,1,0:T(8,128)}, f32[8,768]{1,0:T(8,12...) custom-call(s32[1]{0:T(128)} %bitcast.19.place_ref, ...), custom_call_target="tpu_custom_call" | custom-call | flops 1024 | bytes 1024 | tf_op jit(solution)/shard_map/assemble/pallas_call | solution.py:939
  (68 shorter events, 4.0 us)
Async XLA Ops:
  14.5 5.3 %copy-start.18 = (bf16[768,8]{0,1:T(8,128)(2,1)S(1)}, bf16[768,8]{0,1:T(8,128)(2,1)}, u32[]{:S(2)}) copy-start(bf16[768,8]{0,1:T(8,128)(2,1)} %param.32) | copy-start | bytes 36868
  14.5 43.2 %all-to-all-start = ((bf16[8,256,768]{2,1,0:T(8,128)(2,1)}), bf16[8,256,768]{2,1,0:T(8,128)(2,1)S(1)}, u32[]{:S(2)}, u32[]{:S(2)}) async-start(bf16[8,256,768]{2,1,0:T(8,128)(2,1)} %bitcast.64), calls=%async_computation | async-start | bytes 6291456 | tf_op jit(solution)/shard_map/all_to_all | solution.py:814
  57.7 1.7 copy-start.1
  59.4 43.6 %all-to-all-start.1 = ((bf16[8,272,768]{2,1,0:T(8,128)(2,1)}), bf16[8,272,768]{2,1,0:T(8,128)(2,1)S(1)}, u32[]{:S(2)}, u32[]{:S(2)}) async-start(bf16[8,272,768]{2,1,0:T(8,128)(2,1)} %bitcast.54), calls=%async_computation.1 | async-start | bytes 6684672 | tf_op jit(solution)/shard_map/all_to_all | solution.py:814
  63.1 290.7 %reduce-scatter.2.cloned.1.call-start = ((), (), s32[]{:S(2)}) async-start(), calls=%async_computation.7 | async-start | bytes 11919360 | tf_op jit(solution)/shard_map/reduce_scatter | solution.py:1030
  103.0 1.7 copy-start.3
  173.7 43.6 %all-to-all-start.2 = ((bf16[8,272,768]{2,1,0:T(8,128)(2,1)}), bf16[8,272,768]{2,1,0:T(8,128)(2,1)S(1)}, u32[]{:S(2)}, u32[]{:S(2)}) async-start(bf16[8,272,768]{2,1,0:T(8,128)(2,1)} %bitcast.53), calls=%async_computation.2 | async-start | bytes 6684672 | tf_op jit(solution)/shard_map/all_to_all | solution.py:814
  217.3 1.7 copy-start
  236.6 21.4 %all-to-all-start.3 = ((bf16[8,96,768]{2,1,0:T(8,128)(2,1)}), bf16[8,96,768]{2,1,0:T(8,128)(2,1)S(1)}, u32[]{:S(2)}, u32[]{:S(2)}) async-start(bf16[8,96,768]{2,1,0:T(8,128)(2,1)} %bitcast.61), calls=%async_computation.3 | async-start | bytes 2359296 | tf_op jit(solution)/shard_map/all_to_all | solution.py:840
  258.0 1.0 copy-start.5
  259.0 33.3 %all-to-all-start.4 = ((bf16[8,96,1152]{2,1,0:T(8,128)(2,1)}), bf16[8,96,1152]{2,1,0:T(8,128)(2,1)S(1)}, u32[]{:S(2)}, u32[]{:S(2)}) async-start(bf16[8,96,1152]{2,1,0:T(8,128)(2,1)} %bitcast.58), calls=%async_computation.4 | async-start | bytes 3538944 | tf_op jit(solution)/shard_map/all_to_all | solution.py:840
  292.3 1.2 copy-start.7
  293.5 5.4 %copy-start.2 = (bf16[768,1280]{1,0:T(8,128)(2,1)S(1)}, bf16[768,1280]{1,0:T(8,128)(2,1)}, u32[]{:S(2)}) copy-start(bf16[768,1280]{1,0:T(8,128)(2,1)} %together.14) | copy-start | bytes 5898244
  295.9 3.0 collective-permute-start
  296.4 9.2 %copy-start.6 = (bf16[8,96,768]{2,1,0:T(8,128)(2,1)S(1)}, bf16[8,96,768]{2,1,0:T(8,128)(2,1)}, u32[]{:S(2)}) copy-start(bf16[8,96,768]{2,1,0:T(8,128)(2,1)} %copy-done.5) | copy-start | bytes 3538948
  300.3 0.9 copy-start.10
  301.3 4.5 %copy-start.8 = (bf16[8,96,1152]{2,1,0:T(8,128)(2,1)S(1)}, bf16[8,96,1152]{2,1,0:T(8,128)(2,1)}, u32[]{:S(2)}) copy-start(bf16[8,96,1152]{2,1,0:T(8,128)(2,1)} %copy-done.7) | copy-start | bytes 5308420
  302.1 9.1 %collective-permute-start.1 = (bf16[1,96,1280]{2,1,0:T(8,128)(2,1)}, bf16[1,96,1280]{2,1,0:T(8,128)(2,1)}, u32[]{:S(2)}, u32[]{:S(2)}) collective-permute-start(bf16[1,96,1280]{2,1,0:T(8,128)(2,1)} %get-tuple-element.142), channel_id=1, source_target_pairs={{0,2},{1,3},{2,0},{3,1},{4,6},{5,7},{6,4},{7,5},{8,10},{9,11},{10,... | collective-permute-start | bytes 737288 | tf_op jit(solution)/shard_map/ppermute | solution.py:855
  304.0 13.3 %collective-permute-start.2 = (bf16[1,96,1280]{2,1,0:T(8,128)(2,1)}, bf16[1,96,1280]{2,1,0:T(8,128)(2,1)}, u32[]{:S(2)}, u32[]{:S(2)}) collective-permute-start(bf16[1,96,1280]{2,1,0:T(8,128)(2,1)} %get-tuple-element.144), channel_id=1, source_target_pairs={{0,4},{1,5},{2,6},{3,7},{4,0},{5,1},{6,2},{7,3},{8,12},{9,13},{10,... | collective-permute-start | bytes 737288 | tf_op jit(solution)/shard_map/ppermute | solution.py:855
  305.5 11.8 %collective-permute-start.3 = (bf16[1,96,1280]{2,1,0:T(8,128)(2,1)S(1)}, bf16[1,96,1280]{2,1,0:T(8,128)(2,1)}, u32[]{:S(2)}, u32[]{:S(2)}) collective-permute-start(bf16[1,96,1280]{2,1,0:T(8,128)(2,1)S(1)} %get-tuple-element.143), channel_id=1, source_target_pairs={{0,6},{1,7},{2,4},{3,5},{4,2},{5,3},{6,0},{7,1},{8,14},{9,15},{10,... | collective-permute-start | bytes 737288 | tf_op jit(solution)/shard_map/ppermute | solution.py:855
  318.7 2.4 copy-start.13
  319.5 1.6 copy-start.11
  319.5 14.7 %collective-permute-start.4 = (bf16[96,1536]{1,0:T(8,128)(2,1)}, bf16[96,1536]{1,0:T(8,128)(2,1)}, u32[]{:S(2)}, u32[]{:S(2)}) collective-permute-start(bf16[96,1536]{1,0:T(8,128)(2,1)} %get-tuple-element.115), channel_id=1, source_target_pairs={{0,8},{8,0},{16,24},{24,16},{1,9},{9,1},{17,25},{25,17},{2,10},{10... | collective-permute-start | bytes 884744 | tf_op jit(solution)/shard_map/ppermute | solution.py:820
  321.1 16.1 %collective-permute-start.5 = (bf16[96,1664]{1,0:T(8,128)(2,1)S(1)}, bf16[96,1664]{1,0:T(8,128)(2,1)}, u32[]{:S(2)}, u32[]{:S(2)}) collective-permute-start(bf16[96,1664]{1,0:T(8,128)(2,1)S(1)} %copy-done.11), channel_id=1, source_target_pairs={{0,16},{8,24},{16,0},{24,8},{1,17},{9,25},{17,1},{25,9},{2,18},{10... | collective-permute-start | bytes 958472 | tf_op jit(solution)/shard_map/ppermute | solution.py:820
  323.8 52.8 %all-to-all-start.5 = ((bf16[8,256,768]{2,1,0:T(8,128)(2,1)}), bf16[8,256,768]{2,1,0:T(8,128)(2,1)S(1)}, u32[]{:S(2)}, u32[]{:S(2)}) async-start(bf16[8,256,768]{2,1,0:T(8,128)(2,1)} %bitcast.42), calls=%async_computation.5 | async-start | bytes 6291456 | tf_op jit(solution)/shard_map/all_to_all | solution.py:814
  339.1 12.9 %collective-permute-start.7 = (bf16[96,1664]{1,0:T(8,128)(2,1)}, bf16[96,1664]{1,0:T(8,128)(2,1)S(1)}, u32[]{:S(2)}, u32[]{:S(2)}) collective-permute-start(bf16[96,1664]{1,0:T(8,128)(2,1)} %get-tuple-element.120), channel_id=1, source_target_pairs={{0,8},{8,0},{16,24},{24,16},{1,9},{9,1},{17,25},{25,17},{2,10},{10... | collective-permute-start | bytes 958472 | tf_op jit(solution)/shard_map/ppermute | solution.py:820
  339.4 18.3 %collective-permute-start.6 = (bf16[96,1536]{1,0:T(8,128)(2,1)}, bf16[96,1536]{1,0:T(8,128)(2,1)}, u32[]{:S(2)}, u32[]{:S(2)}) collective-permute-start(bf16[96,1536]{1,0:T(8,128)(2,1)} %get-tuple-element.117), channel_id=1, source_target_pairs={{0,16},{8,24},{16,0},{24,8},{1,17},{9,25},{17,1},{25,9},{2,18},{10... | collective-permute-start | bytes 884744 | tf_op jit(solution)/shard_map/ppermute | solution.py:820
  357.8 1.0 copy-start.12
  360.5 10.4 %collective-permute-start.8 = (bf16[1,1,96,1536]{3,2,1,0:T(8,128)(2,1)}, bf16[1,1,96,1536]{3,2,1,0:T(8,128)(2,1)S(1)}, u32[]{:S(2)}, u32[]{:S(2)}) collective-permute-start(bf16[1,1,96,1536]{3,2,1,0:T(8,128)(2,1)} %get-tuple-element.121), channel_id=1, source_target_pairs={{0,2},{1,3},{2,0},{3,1},{4,6},{5,7},{6,4},{7,5},{8,10},{9,11},{10,... | collective-permute-start | bytes 884744 | tf_op jit(solution)/shard_map/ppermute | solution.py:820
  362.1 10.6 %collective-permute-start.9 = (bf16[1,1,96,1664]{3,2,1,0:T(8,128)(2,1)}, bf16[1,1,96,1664]{3,2,1,0:T(8,128)(2,1)S(1)}, u32[]{:S(2)}, u32[]{:S(2)}) collective-permute-start(bf16[1,1,96,1664]{3,2,1,0:T(8,128)(2,1)} %get-tuple-element.122), channel_id=1, source_target_pairs={{0,4},{1,5},{2,6},{3,7},{4,0},{5,1},{6,2},{7,3},{8,12},{9,13},{10,... | collective-permute-start | bytes 958472 | tf_op jit(solution)/shard_map/ppermute | solution.py:820
  374.6 16.2 %collective-permute-start.11 = (bf16[2,1,96,1664]{3,2,1,0:T(8,128)(2,1)}, bf16[2,1,96,1664]{3,2,1,0:T(8,128)(2,1)}, u32[]{:S(2)}, u32[]{:S(2)}) collective-permute-start(bf16[2,1,96,1664]{3,2,1,0:T(8,128)(2,1)} %get-tuple-element.124), channel_id=1, source_target_pairs={{0,2},{1,3},{2,0},{3,1},{4,6},{5,7},{6,4},{7,5},{8,10},{9,11},{10,... | collective-permute-start | bytes 1916936 | tf_op jit(solution)/shard_map/ppermute | solution.py:820
  374.9 14.8 %collective-permute-start.10 = (bf16[1,2,96,1536]{3,2,1,0:T(8,128)(2,1)}, bf16[1,2,96,1536]{3,2,1,0:T(8,128)(2,1)}, u32[]{:S(2)}, u32[]{:S(2)}) collective-permute-start(bf16[1,2,96,1536]{3,2,1,0:T(8,128)(2,1)} %get-tuple-element.123), channel_id=1, source_target_pairs={{0,4},{1,5},{2,6},{3,7},{4,0},{5,1},{6,2},{7,3},{8,12},{9,13},{10,... | collective-permute-start | bytes 1769480 | tf_op jit(solution)/shard_map/ppermute | solution.py:820
  376.6 1.6 copy-start.4
  389.6 1.2 copy-start.9
  389.6 4.6 %collective-permute-start.14 = (bf16[2,96,1664]{2,1,0:T(8,128)(2,1)}, bf16[2,96,1664]{2,1,0:T(8,128)(2,1)S(1)}, u32[]{:S(2)}, u32[]{:S(2)}) collective-permute-start(bf16[2,96,1664]{2,1,0:T(8,128)(2,1)} %bitcast.25.refs_2_), channel_id=1, source_target_pairs={{0,1},{1,0},{2,3},{3,2},{4,5},{5,4},{6,7},{7,6},{8,9},{9,8},{10,11... | collective-permute-start | bytes 1916936 | tf_op jit(solution)/shard_map/ppermute | solution.py:820
  390.8 4.0 collective-permute-start.15
  390.8 3.4 collective-permute-start.12
  391.3 3.5 collective-permute-start.13
  394.2 0.8 copy-start.16
  394.2 1.1 copy-start.14
  394.8 0.8 copy-start.17
  394.8 1.0 copy-start.15
Sparse Core Ops, SparseCore 0:
  158.3 162.5 reduce-scatter.1
